TPU v7x, 32 devices: a whole 2x2x4 slice. The times are simulated.
32 devices in a mesh: groups: 2 (over y), seg: 4 (over z), slab: 2 (over x), comp: 2 (over core).
Axes of the slice: x: 2, y: 2, z: 4, core: 2. Of those that a mesh axis runs over, the one named last changes fastest.
Arguments:
- base: float32 [8, 3, 64, 4096], P(('groups', 'seg'), None, 'slab'), parts along dimension 0, may hold values from -6 to 6
- state: float32 [8, 2, 3, 64, 4096], P(('groups', 'seg'), 'comp', None, 'slab'), parts along dimension 0, may hold values from -6 to 6
- wavenumber: int32 [2], P('groups'), parts along dimension 0, may hold values from 1 to 4
- cutoff: int32 [6], P('groups'), parts along dimension 0, may hold values from 18 to 21, as said below
Outputs:
- base_gap: float32 [8, 3, 64, 4096], P(('groups', 'seg'), None, ('slab', 'comp')), parts along dimension 0
- state_gap: float32 [8, 2, 3, 64, 4096], P(('groups', 'seg'), 'comp', None, 'slab'), parts along dimension 0
There are 2 independent parts, one for each index of `groups`. A program takes and returns all parts, laid end to end along the dimension named above; each array names one. Nothing has to cross between parts.
Inputs may be any that keep to these rules, and one draw needn't show every extreme that they name: `cutoff`: each entry is at most one third of 64, rounded down, and at least that minus three; one entry always equals it.
All inputs are finite; a program needn't handle non-finite values.
Results may differ from a plain program's by a relative error of at most 0.0001.
Values sent between devices are 32-bit elements; how exact they have to be, the bound alone decides.
A program may use at most 128 MiB of HBM per device.

v0:
```python
import functools

import jax
import jax.numpy as jnp
import ml_dtypes
import numpy as np
from jax import lax
from jax.experimental import pallas as pl
from jax.experimental.pallas import tpu as pltpu
from jax.sharding import PartitionSpec as P

N = 64
BACK, GRID, AHEAD, SPEC, Z1, Z2, Z3, Y1 = 4, 4, 4, 4, 8, 4, 8, 6
THIRD = N // 3
LOW = THIRD - 3
KZ = THIRD + 1
KP = 24
MP = 48
PAIRS = N // 2
FLUX = 14 * 10**9
HALF = KZ // 2
viscosity = 0.025
time_step = 0.02
forcing_amp = 10.0
f32 = jnp.float32
bf16 = jnp.bfloat16

NN = (((1,), (0,)), ((), ()))
NT = (((1,), (1,)), ((), ()))


def split(value):
    high = value.astype(bf16)
    return high, (value - high.astype(f32)).astype(bf16)


def dot3(left, right, dims):
    dot = functools.partial(lax.dot_general, dimension_numbers=dims, preferred_element_type=f32)
    return dot(left[0], right[0]) + (dot(left[0], right[1]) + dot(left[1], right[0]))


def table(values):
    values = np.asarray(values, np.float32)
    high = values.astype(ml_dtypes.bfloat16)
    low = (values - high.astype(np.float32)).astype(ml_dtypes.bfloat16)
    return np.stack([high, low], axis=-3)


def table3(values):
    high, low = np.moveaxis(table(values), -3, 0)
    return np.concatenate([high, high, low], axis=-1)


def left3(left, value, dims):
    high, low = split(value)
    deep = jnp.concatenate([high, low, high], axis=dims[0][1][0])
    return lax.dot_general(left, deep, dimension_numbers=dims, preferred_element_type=f32)


def signed():
    m = np.arange(2 * THIRD + 1)
    return np.where(m <= THIRD, m, m - (2 * THIRD + 1))


def angles(first, second):
    return np.mod(np.outer(first, second), N) * (2 * np.pi / N)


def cuts():
    return range(LOW, THIRD + 1)


def z_tables():
    plain, ik = [], []
    k = np.arange(KZ)
    a = angles(k, np.arange(N))
    for cut in cuts():
        keep = 1.0 * (k <= cut)[:, None]
        w = np.zeros((2, KP, N))
        v = np.zeros((2, KP, N))
        w[0, :KZ], w[1, :KZ] = keep * np.cos(a), -keep * np.sin(a)
        v[0, :KZ], v[1, :KZ] = keep * k[:, None] * np.sin(a), keep * k[:, None] * np.cos(a)
        plain.append(np.kron(np.eye(2), w.reshape(2 * KP, N)))
        ik.append(np.kron(np.eye(2), v.reshape(2 * KP, N)))
    return table3(np.stack([np.stack(plain), np.stack(ik)], axis=1))


def y_tables():
    out = []
    m = signed()
    count = len(m)
    a = angles(m, np.arange(N))
    for cut in cuts():
        keep = 1.0 * (np.abs(m) <= cut)[:, None]
        c, s = keep * np.cos(a), keep * np.sin(a)
        w = np.zeros((2, MP, N, 2))
        w[0, :count, :, 0], w[0, :count, :, 1] = c, s
        w[1, :count, :, 0], w[1, :count, :, 1] = -s, c
        v = np.zeros_like(w)
        v[0, :count] = -m[:, None, None] * w[1, :count]
        v[1, :count] = m[:, None, None] * w[0, :count]
        out.append(np.stack([w.reshape(2 * MP, 2 * N), v.reshape(2 * MP, 2 * N)]))
    return table3(np.stack(out))


def y_back():
    m = signed()
    count = len(m)
    a = angles(np.arange(N), m)
    c, s = np.cos(a) / N, np.sin(a) / N
    w = np.zeros((N, 2, 2, MP))
    w[:, 0, 0, :count], w[:, 0, 1, :count] = c, -s
    w[:, 1, 0, :count], w[:, 1, 1, :count] = s, c
    v = np.zeros_like(w)
    v[:, :, 0, :count] = m * w[:, :, 1, :count]
    v[:, :, 1, :count] = -m * w[:, :, 0, :count]
    return table3(np.stack([w.reshape(2 * N, 2 * MP), v.reshape(2 * N, 2 * MP)]))


def z_back():
    k = np.arange(KZ)
    a = angles(k, np.arange(N))
    weight = (np.where(k == 0, 1.0, 2.0) / N)[:, None]
    w = np.zeros((2, KP, N))
    w[0, :KZ], w[1, :KZ] = weight * np.cos(a), -weight * np.sin(a)
    v = np.zeros_like(w)
    v[0, :KZ] = k[:, None] * w[1, :KZ]
    v[1, :KZ] = -k[:, None] * w[0, :KZ]
    pair = lambda t: np.kron(np.eye(2), t.reshape(2 * KP, N))
    return table3(np.stack([pair(w).T, pair(v).T]))


def x_filters(slabs):
    rows = N // slabs
    out = []
    x = np.arange(N)
    for cut in cuts():
        n = np.arange(-cut, cut + 1)
        d = np.mod(x[:, None] - x[None, :], N)
        phase = 2 * np.pi / N * n[:, None, None] * -d
        plain = np.cos(phase).sum(0) / N
        deriv = (-n[:, None, None] * np.sin(phase)).sum(0) / N
        both = np.stack([plain, deriv]).reshape(2, slabs, rows, slabs, rows)
        wide = np.zeros((slabs, 2, slabs, 3, rows, 3, rows))
        for i in range(3):
            wide[:, :, :, i, :, i, :] = both.transpose(3, 0, 1, 2, 4)
        out.append(wide.reshape(slabs, 2, slabs, 3 * rows, 3 * rows))
    return table(np.stack(out))


def x_tables(slabs):
    rows = N // slabs
    n = signed()
    count = len(n)
    a = angles(np.arange(N), n).reshape(slabs, rows, count)
    out = []
    for cut in cuts():
        keep = 1.0 * (np.abs(n) <= cut)
        c, s = np.cos(a) * keep, np.sin(a) * keep
        w = np.zeros((slabs, 2, 2, 3, rows, 3, 2, 64))
        for i in range(3):
            w[:, 0, 0, i, :, i, 0, :count] = c
            w[:, 0, 0, i, :, i, 1, :count] = -s
            w[:, 0, 1, i, :, i, 0, :count] = s
            w[:, 0, 1, i, :, i, 1, :count] = c
        w[:, 1, :, :, :, :, 0, :count] = -n * w[:, 0, :, :, :, :, 1, :count]
        w[:, 1, :, :, :, :, 1, :count] = n * w[:, 0, :, :, :, :, 0, :count]
        out.append(w.reshape(slabs, 2, 2, 3 * rows, 384))
    return table(np.stack(out))


def x_back(slabs):
    rows = N // slabs
    n = signed()
    count = len(n)
    a = angles(n, np.arange(N)).reshape(count, slabs, rows).transpose(1, 0, 2)
    c, s = np.cos(a) / N, np.sin(a) / N
    w = np.zeros((slabs, 2, 3, 2, 64, 3, rows))
    for i in range(3):
        w[:, 0, i, 0, :count, i] = c
        w[:, 0, i, 1, :count, i] = -s
        w[:, 1, i, 0, :count, i] = s
        w[:, 1, i, 1, :count, i] = c
    return table(w.reshape(slabs, 2, 384, 3 * rows))


def both(ref, *index):
    return ref[(*index, 0)], ref[(*index, 1)]


def lanes(p):
    return pl.ds(pl.multiple_of(p * 128, 128), 128)


def pair_rows(p):
    return pl.ds(pl.multiple_of(p * 4 * KP, 8), 4 * KP)


def column(k):
    return pl.ds(k, 2 * N, stride=KP)


def flat(block):
    return block.reshape(block.shape[0] * block.shape[1], block.shape[2])


def loop(count, unroll, step):
    def go(i, carry):
        step(i)
        return carry

    lax.fori_loop(0, count, go, 0, unroll=unroll)


def clear_padding(*works):
    for k in range(KZ, KP):
        for work in works:
            work[column(k), :] = jnp.zeros((2 * N, work.shape[1]), f32)


def base_ahead(base_ref, wz_ref, wy_ref, out_ref, half_ref, work):
    def along_z(p):
        work[pair_rows(p), :] = left3(wz_ref[0], flat(base_ref[:, :, lanes(p)]), NT)

    loop(PAIRS, Z1, along_z)

    def along_y(k):
        out_ref[k] = left3(wy_ref[0], work[column(k), :], NN)

    loop(KZ, Y1, along_y)
    first = HALF * lax.axis_index("comp")

    def share(j):
        half_ref[j] = out_ref[first + j]

    loop(HALF, 1, share)


def sign_step():
    return jnp.where(lax.axis_index("comp") == 0, -time_step, time_step).astype(f32)


def flux_ahead(base_ref, state_ref, wz_ref, wy_ref, g_ref, work_a, work_b):
    scale = sign_step()

    def along_z(p):
        state = state_ref[:, :, lanes(p)]
        scaled = state * scale
        f1, f2 = (flat(scaled * base_ref[j, :, lanes(p)][None]) for j in (1, 2))
        plain = wz_ref[0]
        work_a[pair_rows(p), :] = left3(plain, flat(state), NT) + left3(wz_ref[1], f2, NT)
        work_b[pair_rows(p), :] = left3(plain, f1, NT)

    loop(PAIRS, Z2, along_z)

    def along_y(k):
        g_ref[k] = left3(wy_ref[0], work_a[column(k), :], NN) + left3(
            wy_ref[1], work_b[column(k), :], NN
        )

    loop(KZ, Y1, along_y)


def flux_x_ahead(base_ref, state_ref, wz_ref, wy_ref, f_ref, work):
    scale = sign_step()

    def along_z(p):
        f0 = flat(state_ref[:, :, lanes(p)] * scale * base_ref[0, :, lanes(p)][None])
        work[pair_rows(p), :] = left3(wz_ref[0], f0, NT)

    loop(PAIRS, Z2, along_z)

    def along_y(k):
        f_ref[k] = left3(wy_ref[0], work[column(k), :], NN)

    loop(KZ, Y1, along_y)


def gradients(
    slabs, count, *refs,
):
    got, rest = refs[:count], refs[count:]
    side = lax.axis_index("comp")
    if count == 1:
        visits = [(lambda j: (j, [got[0][s, j] for s in range(slabs)]), KZ)]
    else:
        own, mine, partner = got

        def visit(ref, first):
            return lambda j: (first + j, [own[first + j], ref[j]])

        visits = [
            (visit(mine, HALF * side), HALF),
            (visit(partner, HALF * (1 - side)), HALF),
        ]
    gradients_of(slabs, visits, *rest)


def gradients_of(
    slabs, visits, base_ref, state_ref, force_ref, pd_ref, yb_ref, zb_ref, wz_ref, wy_ref,
    xt_ref, base_out_ref, coupled_ref, work_0, work_1, work_2,
):
    tangent = lax.axis_index("comp") == 0

    def back_y(visit, j):
        k, sources = visit(j)
        sources = [split(source) for source in sources]

        def across(kind):
            total = dot3(sources[0], both(pd_ref, kind, 0), NN)
            for s in range(1, slabs):
                total = total + dot3(sources[s], both(pd_ref, kind, s), NN)
            return total

        plain, deriv = across(0), across(1)
        work_0[column(k), :] = left3(yb_ref[0], deriv, NN)
        work_1[column(k), :] = left3(yb_ref[1], plain, NN)
        work_2[column(k), :] = left3(yb_ref[0], plain, NN)

    clear_padding(work_0, work_1, work_2)
    for visit, count in visits:
        loop(count, BACK, functools.partial(back_y, visit))

    def grid_space(p):
        state = state_ref[:, :, lanes(p)]
        base = base_ref[:, :, lanes(p)]
        grad = []
        for work, kind in ((work_0, 0), (work_1, 0), (work_2, 1)):
            rows = left3(zb_ref[kind], work[pair_rows(p), :], NN).T
            grad.append(rows.reshape(base.shape))
        coupled, driven = [], []
        for i in range(3):
            total = 0.0
            drive = 0.0
            for j in range(3):
                total = total + jnp.where(tangent, grad[j][i], grad[i][j]) * state[j]
                drive = drive + grad[j][i] * base[j]
            if i == 0:
                drive = drive - force_ref[:, lanes(p)]
            coupled.append(-time_step * total)
            driven.append(base[i] - time_step * drive)
        plain = wz_ref[0]
        coupled_ref[pair_rows(p), :] = left3(plain, jnp.concatenate(coupled, axis=0), NT)
        work_1[pair_rows(p), :] = left3(plain, jnp.concatenate(driven, axis=0), NT)

    loop(PAIRS, GRID, grid_space)

    waves = plane_waves()
    first = HALF * lax.axis_index("comp")

    def base_ahead_x(step):
        j = HALF - 1 - step
        k = first + j
        driven = left3(wy_ref[0], work_1[column(k), :], NN)
        modes = 0.0
        for d in range(2):
            rows = slice(d * MP, (d + 1) * MP)
            modes = modes + dot3(split(driven[rows]), both(xt_ref, 0, d), NN)
        emit(waves, base_out_ref, j, HALF, modes, k)

    loop(HALF, AHEAD, base_ahead_x)


def emit(waves, ref, slot, last, modes, k):
    new = projected(waves, modes, k)
    ref[slot] = jnp.concatenate(new[:2], axis=1)
    ref[last] = jnp.concatenate([new[2], jnp.zeros_like(new[2])], axis=1)


def state_ahead_x(coupled_ref, wy_ref, xt_ref, g_ref, f_ref, out_ref):
    waves = plane_waves()

    def ahead_x(step):
        k = KZ - 1 - step
        total = g_ref[k] + left3(wy_ref[0], coupled_ref[column(k), :], NN)
        outer = f_ref[k]
        modes = 0.0
        for d in range(2):
            rows = slice(d * MP, (d + 1) * MP)
            modes = modes + dot3(split(total[rows]), both(xt_ref, 0, d), NN)
            modes = modes + dot3(split(outer[rows]), both(xt_ref, 1, d), NN)
        emit(waves, out_ref, k, KZ, modes, k)

    loop(KZ, AHEAD, ahead_x)


def plane_waves():
    column_n = lax.rem(lax.broadcasted_iota(jnp.int32, (MP, 128), 1), 64)
    row_m = lax.broadcasted_iota(jnp.int32, (MP, 128), 0)
    wrap = lambda v: jnp.where(v <= THIRD, v, v - (2 * THIRD + 1)).astype(f32)
    return wrap(column_n), wrap(row_m)


def projected(waves, modes, k):
    wave_x, wave_y = waves
    wave_z = jnp.asarray(k, jnp.int32).astype(f32)
    square = wave_x * wave_x + wave_y * wave_y + wave_z * wave_z
    safe = jnp.where(square > 0, square, 1.0)
    damping = 1.0 / (1.0 + viscosity * time_step * square)
    w = [modes[:, i * 128 : (i + 1) * 128] for i in range(3)]
    divergence = (wave_x * w[0] + wave_y * w[1] + wave_z * w[2]) / safe
    return [
        damping * (w[0] - wave_x * divergence),
        damping * (w[1] - wave_y * divergence),
        damping * (w[2] - wave_z * divergence),
    ]


def finish(count, halved, *refs):
    parts, (near_ref, xb_ref, yb_ref, zb_ref, out_ref, work) = refs[:count], refs[count:]
    wave_x, wave_y = plane_waves()
    clear_padding(work)

    def spectral(parts, first, last, j):
        k = first + j
        modes, third = 0.0, 0.0
        for part in parts:
            modes = modes + part[j]
            third = third + part[last, :, :128]
        w0, w1 = modes[:, :128], modes[:, 128:]
        whole = jnp.asarray(k, jnp.int32)
        inverse = 1.0 / jnp.maximum(whole, 1).astype(f32)
        w2 = jnp.where(whole == 0, third, -(wave_x * w0 + wave_y * w1) * inverse)
        new = split(jnp.concatenate([w0, w1, w2], axis=1))
        rows = [dot3(new, both(xb_ref, d), NN) for d in range(2)]
        work[column(k), :] = left3(yb_ref[0], jnp.concatenate(rows, axis=0), NN)

    if halved:
        side = lax.axis_index("comp")
        for part, place in zip(parts, (side, 1 - side)):
            loop(HALF, SPEC, functools.partial(spectral, [part], HALF * place, HALF))
    else:
        loop(KZ, SPEC, functools.partial(spectral, parts, 0, KZ))

    def along_z(p):
        rows = left3(zb_ref[0], work[pair_rows(p), :], NN).T
        near = near_ref[:, :, lanes(p)]
        out_ref[:, :, lanes(p)] = rows.reshape(near.shape) - near

    loop(PAIRS, Z3, along_z)


def call(kernel, out_shape, scratch, cost, *operands):
    return pl.pallas_call(
        kernel,
        out_shape=out_shape,
        in_specs=[pl.BlockSpec(memory_space=pltpu.VMEM)] * len(operands),
        out_specs=jax.tree.map(lambda _: pl.BlockSpec(memory_space=pltpu.VMEM), out_shape),
        scratch_shapes=scratch,
        compiler_params=pltpu.CompilerParams(vmem_limit_bytes=48 * 2**20),
        cost_estimate=pl.CostEstimate(flops=cost, bytes_accessed=2**10, transcendentals=0),
    )(*operands)


def body(base, state, wavenumber, cutoff):
    base, state = base[0], state[0, 0]
    slab_rows = base.shape[1]
    half = slab_rows // lax.axis_size("comp")
    slabs = lax.axis_size("slab")
    segs = lax.axis_size("seg")
    slab = lax.axis_index("slab")
    side = lax.axis_index("comp")
    width = 3 * slab_rows
    which = cutoff - LOW

    route = [((s, 0), ((s - 1) % segs, 0)) for s in range(segs)]
    route += [((s, 1), ((s + 1) % segs, 1)) for s in range(segs)]
    route = [(a * 2 + b, c * 2 + d) for (a, b), (c, d) in route]
    wz = lax.dynamic_index_in_dim(jnp.asarray(z_tables()), which[2], 0, False)
    wy = lax.dynamic_index_in_dim(jnp.asarray(y_tables()), which[1], 0, False)
    filters, ahead = jnp.asarray(x_filters(slabs)), jnp.asarray(x_tables(slabs))
    pick = lambda t: lax.dynamic_slice(
        t, (which[0], slab) + (0,) * (t.ndim - 2), (1, 1) + t.shape[2:]
    )[0, 0]
    pd, xt = pick(filters), pick(ahead)
    xb = lax.dynamic_index_in_dim(jnp.asarray(x_back(slabs)), slab, 0, False)
    yb, zb = jnp.asarray(y_back()), jnp.asarray(z_back())

    modes = jax.ShapeDtypeStruct((KZ, 2 * MP, width), f32)
    half_modes = jax.ShapeDtypeStruct((HALF, 2 * MP, width), f32)
    spectrum = jax.ShapeDtypeStruct((KZ + 1, MP, 256), f32)
    half_spectrum = jax.ShapeDtypeStruct((HALF + 1, MP, 256), f32)
    work = pltpu.VMEM((2 * N * KP, width), f32)
    own, share = call(base_ahead, (modes, half_modes), [work], 4 * 10**9, base, wz, wy)
    later, later_base, share = lax.optimization_barrier((state, base, share))
    near_state = lax.ppermute(later, ("seg", "comp"), route)
    base_half = lax.dynamic_slice_in_dim(later_base, side * half, half, 1)
    near_base = lax.ppermute(base_half, "seg", [((s + 1) % segs, s) for s in range(segs)])
    if slabs == 2:
        other = lax.ppermute(share, "slab", [(0, 1), (1, 0)])
        partner = lax.ppermute(other, "comp", [(0, 1), (1, 0)])
        first = slab == 0
        got = (own, other, partner)
        pd = jnp.where(first, pd, pd[:, ::-1])
    else:
        got = (lax.all_gather(own, "slab"),)
    g = call(flux_ahead, modes, [work] * 2, FLUX, base, state, wz, wy)
    f = call(flux_x_ahead, modes, [work], 10**9, base, state, wz, wy)

    *got, g, f = lax.optimization_barrier((*got, g, f))

    y = jnp.arange(N, dtype=jnp.int32)
    phase = jnp.mod(wavenumber[0] * y, N).astype(f32) * (2.0 * jnp.pi / N)
    force = jnp.repeat(forcing_amp * jnp.sin(phase), N)[None]
    lined = jax.ShapeDtypeStruct((2 * N * KP, width), f32)
    base_modes, coupled = call(
        functools.partial(gradients, slabs, len(got)), (half_spectrum, lined), [work] * 3,
        25 * 10**9, *got, base, state, force, pd, yb, zb, wz, wy, xt,
    )
    state_modes = call(state_ahead_x, spectrum, [], 3 * 10**9, coupled, wy, xt, g, f)
    near_state, near_base, state_modes = lax.optimization_barrier(
        (near_state, near_base, state_modes)
    )
    if slabs == 2:
        swap = lambda v: lax.ppermute(v, "slab", [(0, 1), (1, 0)])
        state_other = swap(state_modes)
        base_other, state_modes = lax.optimization_barrier((swap(base_modes), state_modes))
        base_sum = base_modes + base_other
        state_parts = (state_modes, state_other)
    else:
        base_sum = lax.psum(base_modes, "slab")
        state_parts = (lax.psum(state_modes, "slab"),)
    base_parts = (base_sum, lax.ppermute(base_sum, "comp", [(0, 1), (1, 0)]))

    shape = jax.ShapeDtypeStruct(base.shape, f32)
    last = functools.partial(finish, len(state_parts), False)
    last_base = functools.partial(finish, 2, True)
    near_wide = jnp.concatenate([near_base, near_base], axis=1)
    base_gap = call(last_base, shape, [work], 10**8, *base_parts, near_wide, xb, yb, zb)
    base_gap = lax.dynamic_slice_in_dim(base_gap, side * half, half, 1)
    state_gap = call(last, shape, [work], 10**10, *state_parts, near_state, xb, yb, zb)
    return base_gap[None], state_gap[None, None]


def solution(mesh):
    return jax.shard_map(
        body,
        mesh=mesh,
        in_specs=(
            P(("groups", "seg"), None, "slab", None),
            P(("groups", "seg"), "comp", None, "slab", None),
            P("groups"),
            P("groups"),
        ),
        out_specs=(
            P(("groups", "seg"), None, ("slab", "comp"), None),
            P(("groups", "seg"), "comp", None, "slab", None),
        ),
        check_vma=False,
    )
```

profile of v0, /device:TPU:0, one launch (start us, length us, event | category | flops | bytes accessed | tf_op | source)
XLA Modules:
  0.0 117.1 jit_solution(11660189403005008674)
XLA Ops:
  0.6 0.7 broadcast_add_fusion
  1.3 0.6 fusion.5
  5.8 1.0 dynamic-slice_bitcast_fusion.4
  6.8 1.4 %copy-done = f32[1,3,32,4096]{3,2,1,0:T(8,128)S(1)} copy-done((f32[1,3,32,4096]{3,2,1,0:T(8,128)S(1)}, f32[1,3,32,4096]{3,2,1,0:T(8,128)}, u32[]{:S(2)}) %copy-start) | copy-done | bytes 1572888
  8.2 3.9 %shard_map.122 = (f32[22,96,96]{2,1,0:T(8,128)S(1)}, f32[11,96,96]{2,1,0:T(8,128)}) custom-call(f32[3,32,4096]{2,1,0:T(8,128)S(1)} %bitcast.21, bf16[2,96,384]{2,1,0:T(8,128)(2,1)S(1)} %get-tuple-element.40.wz_ref.refs_9_, bf16[2,96,384]{2,1,0:T(8,128)(2,1)S(1)} %get-tuple-element.39.wy_ref.refs_10_), custom_call_target="tpu_custom_call" | custom-call | flops 4000000000 | bytes 1024 | tf_op jit(solution)/shard_map/pallas_call | solution.py:444
  12.1 1.0 copy-done.9
  13.1 2.9 %collective-permute-start = (f32[11,96,96]{2,1,0:T(8,128)}, f32[11,96,96]{2,1,0:T(8,128)}, u32[]{:S(2)}, u32[]{:S(2)}) collective-permute-start(f32[11,96,96]{2,1,0:T(8,128)} %get-tuple-element.21), channel_id=1, source_target_pairs={{0,2},{2,0},{1,3},{3,1},{4,6},{6,4},{5,7},{7,5},{8,10},{10,8},{9,1... | collective-permute-start | bytes 1216520 | tf_op jit(solution)/shard_map/ppermute | solution.py:490
  16.0 0.9 constant_dynamic-slice_fusion
  17.0 3.6 %collective-permute-start.4 = (f32[3,16,4096]{2,1,0:T(8,128)}, f32[3,16,4096]{2,1,0:T(8,128)}, u32[]{:S(2)}, u32[]{:S(2)}) collective-permute-start(f32[3,16,4096]{2,1,0:T(8,128)} %constant_dynamic-slice_fusion), channel_id=1, source_target_pairs={{4,0},{8,4},{12,8},{0,12},{5,1},{9,5},{13,9},{1,13},{6,2},{10,6},{... | collective-permute-start | bytes 2359304 | tf_op jit(solution)/shard_map/ppermute | solution.py:488
  20.6 0.4 collective-permute-start.3
  21.0 6.5 %shard_map.123.g_ref = f32[22,96,96]{2,1,0:T(8,128)S(1)} custom-call(f32[3,32,4096]{2,1,0:T(8,128)S(1)} %bitcast.23, f32[3,32,4096]{2,1,0:T(8,128)S(1)} %bitcast.27, bf16[2,96,384]{2,1,0:T(8,128)(2,1)S(1)} %get-tuple-element.40.wz_ref.refs_9_, bf16[2,96,384]{2,1,0:T(8,128)(2,1)S(1)} %get-tuple-element.39.wy_ref.refs_10_), custom_call_target="tpu_custom_call" | custom-call | flops 14000000000 | bytes 1024 | tf_op jit(solution)/shard_map/pallas_call | solution.py:444
  27.5 1.0 copy-done.7
  30.8 1.6 %dynamic-slice_bitcast_fusion.3 = bf16[2,2,2,96,96]{4,3,2,1,0:T(8,128)(2,1)} fusion(bf16[4,2,2,2,2,96,96]{6,5,4,3,2,1,0:T(8,128)(2,1)} %constant.63.clone, s32[]{:T(128)S(6)} %select_n.40, s32[]{:T(128)S(6)} %select_n.41), kind=kLoop, calls=%fused_computation.5 | loop fusion | bytes 294920 | tf_op jit(solution)/shard_map/squeeze | solution.py:472
  32.4 3.7 %shard_map.124.f_ref = f32[22,96,96]{2,1,0:T(8,128)S(1)} custom-call(f32[3,32,4096]{2,1,0:T(8,128)S(1)} %bitcast.24, f32[3,32,4096]{2,1,0:T(8,128)S(1)} %bitcast.28, bf16[2,96,384]{2,1,0:T(8,128)(2,1)S(1)} %get-tuple-element.40.wz_ref.refs_9_, bf16[2,96,384]{2,1,0:T(8,128)(2,1)S(1)} %get-tuple-element.39.wy_ref.refs_10_), custom_call_target="tpu_custom_call" | custom-call | flops 1000000000 | bytes 1024 | tf_op jit(solution)/shard_map/pallas_call | solution.py:444
  36.1 1.0 copy-done.3
  37.1 0.1 broadcast_in_dim.9
  37.2 0.1 broadcast_in_dim_reshape.3.refs_5_
  37.3 1.3 %dynamic-slice_bitcast_fusion.1.refs_11_.xt_ref = bf16[2,2,2,96,384]{4,3,2,1,0:T(8,128)(2,1)S(1)} fusion(bf16[4,2,2,2,2,96,384]{6,5,4,3,2,1,0:T(8,128)(2,1)} %constant.64.clone, s32[]{:T(128)S(6)} %select_n.40, s32[]{:T(128)S(6)} %select_n.41), kind=kLoop, calls=%fused_computation.2 | loop fusion | bytes 1179656 | tf_op jit(solution)/shard_map/squeeze | solution.py:472
  38.6 1.1 reverse_select_fusion.refs_6_
  39.7 26.1 %shard_map.125 = (f32[12,48,256]{2,1,0:T(8,128)S(1)}, f32[3072,96]{1,0:T(8,128)S(1)}) custom-call(f32[22,96,96]{2,1,0:T(8,128)S(1)} %copy-done.10, f32[11,96,96]{2,1,0:T(8,128)} %collective-permute-done.refs_1_, f32[11,96,96]{2,1,0:T(8,128)} %collective-permute-done.1.refs_2_, f32[3,32,4096]{2,1,0:T(8,128)} %bitcast.20, f32[3,32,4096]{2,1,0:T(8,128)} %bitcast.25, ...), custom_call_target="tpu_custom_call" | custom-call | flops 24999999488 | bytes 1024 | tf_op jit(solution)/shard_map/pallas_call | solution.py:444
  65.8 0.7 collective-permute-start.2
  66.5 7.8 %shard_map.126.refs_0_ = f32[23,48,256]{2,1,0:T(8,128)S(1)} custom-call(f32[3072,96]{1,0:T(8,128)S(1)} %get-tuple-element.28.coupled_ref, bf16[2,96,384]{2,1,0:T(8,128)(2,1)S(1)} %get-tuple-element.39.wy_ref.refs_10_, bf16[2,2,2,96,384]{4,3,2,1,0:T(8,128)(2,1)S(1)} %dynamic-slice_bitcast_fusion.1.refs_11_.xt_ref, f32[22,96,96]{2,1,0:T(8,128)S(1)} %copy-done.8, ...), custom_call_target="tpu_custom_call" | custom-call | flops 3000000000 | bytes 1024 | tf_op jit(solution)/shard_map/pallas_call | solution.py:444
  74.4 1.5 %collective-permute-start.6 = (f32[23,48,256]{2,1,0:T(8,128)S(1)}, f32[23,48,256]{2,1,0:T(8,128)S(1)}, u32[]{:S(2)}, u32[]{:S(2)}) collective-permute-start(f32[23,48,256]{2,1,0:T(8,128)S(1)} %shard_map.126.refs_0_), channel_id=1, source_target_pairs={{0,2},{2,0},{1,3},{3,1},{4,6},{6,4},{5,7},{7,5},{8,10},{10,8},{9,1... | collective-permute-start | bytes 3391496 | tf_op jit(solution)/shard_map/ppermute | solution.py:515
  75.9 6.2 %collective-permute-done.2 = f32[12,48,256]{2,1,0:T(8,128)S(1)} collective-permute-done((f32[12,48,256]{2,1,0:T(8,128)S(1)}, f32[12,48,256]{2,1,0:T(8,128)S(1)}, u32[]{:S(2)}, u32[]{:S(2)}) %collective-permute-start.2) | collective-permute-done | bytes 589856 | tf_op jit(solution)/shard_map/ppermute | solution.py:515
  82.0 0.1 add.37.refs_0_
  82.1 0.1 collective-permute-start.5
  82.2 1.5 %pad_maximum_fusion.refs_2_ = f32[3,32,4096]{2,1,0:T(8,128)S(1)} fusion(f32[3,16,4096]{2,1,0:T(8,128)} %collective-permute-done.4), kind=kLoop, calls=%fused_computation | loop fusion | flops 393216 | bytes 2359296 | tf_op jit(solution)/shard_map/concatenate | solution.py:528
  83.7 0.5 collective-permute-done.5.refs_1_
  84.2 9.2 %shard_map.127 = f32[3,32,4096]{2,1,0:T(8,128)S(1)} custom-call(f32[12,48,256]{2,1,0:T(8,128)S(1)} %add.37.refs_0_, f32[12,48,256]{2,1,0:T(8,128)S(1)} %collective-permute-done.5.refs_1_, f32[3,32,4096]{2,1,0:T(8,128)S(1)} %pad_maximum_fusion.refs_2_, bf16[2,2,384,96]{3,2,1,0:T(8,128)(2,1)S(1)} %dynamic-slice_bitcast_fusion.2.refs_3_, ...), custom_call_target="tpu_custom_call" | custom-call | flops 100000000 | bytes 1024 | tf_op jit(solution)/shard_map/pallas_call | solution.py:444
  93.4 0.9 dynamic-slice_bitcast_fusion
  94.3 11.5 %collective-permute-done.6.refs_1_ = f32[23,48,256]{2,1,0:T(8,128)S(1)} collective-permute-done((f32[23,48,256]{2,1,0:T(8,128)S(1)}, f32[23,48,256]{2,1,0:T(8,128)S(1)}, u32[]{:S(2)}, u32[]{:S(2)}) %collective-permute-start.6) | collective-permute-done | bytes 1130528 | tf_op jit(solution)/shard_map/ppermute | solution.py:515
  105.9 11.2 %shard_map.128 = f32[3,32,4096]{2,1,0:T(8,128)} custom-call(f32[23,48,256]{2,1,0:T(8,128)S(1)} %shard_map.126.refs_0_, f32[23,48,256]{2,1,0:T(8,128)S(1)} %collective-permute-done.6.refs_1_, f32[3,32,4096]{2,1,0:T(8,128)} %collective-permute-done.3.refs_2_, bf16[2,2,384,96]{3,2,1,0:T(8,128)(2,1)S(1)} %dynamic-slice_bitcast_fusion.2.refs_3_, ...), custom_call_target="tpu_custom_call" | custom-call | flops 10000000000 | bytes 1024 | tf_op jit(solution)/shard_map/pallas_call | solution.py:444
  (27 shorter events, 0.1 us)
Async XLA Ops:
  6.8 1.4 %copy-start = (f32[1,3,32,4096]{3,2,1,0:T(8,128)S(1)}, f32[1,3,32,4096]{3,2,1,0:T(8,128)}, u32[]{:S(2)}) copy-start(f32[1,3,32,4096]{3,2,1,0:T(8,128)} %param.11) | copy-start | bytes 4718596
  8.2 7.8 %copy-start.1 = (f32[1,3,32,4096]{3,2,1,0:T(8,128)S(1)}, f32[1,3,32,4096]{3,2,1,0:T(8,128)}, u32[]{:S(2)}) copy-start(f32[1,3,32,4096]{3,2,1,0:T(8,128)} %param.11) | copy-start | bytes 4718596
  12.1 1.0 copy-start.9
  13.1 7.5 %copy-start.2 = (f32[1,1,3,32,4096]{4,3,2,1,0:T(8,128)S(1)}, f32[1,1,3,32,4096]{4,3,2,1,0:T(8,128)}, u32[]{:S(2)}) copy-start(f32[1,1,3,32,4096]{4,3,2,1,0:T(8,128)} %param.12) | copy-start | bytes 4718596
  13.1 19.3 %collective-permute-start = (f32[11,96,96]{2,1,0:T(8,128)}, f32[11,96,96]{2,1,0:T(8,128)}, u32[]{:S(2)}, u32[]{:S(2)}) collective-permute-start(f32[11,96,96]{2,1,0:T(8,128)} %get-tuple-element.21), channel_id=1, source_target_pairs={{0,2},{2,0},{1,3},{3,1},{4,6},{6,4},{5,7},{7,5},{8,10},{10,8},{9,1... | collective-permute-start | bytes 1216520 | tf_op jit(solution)/shard_map/ppermute | solution.py:490
  17.0 57.4 %collective-permute-start.4 = (f32[3,16,4096]{2,1,0:T(8,128)}, f32[3,16,4096]{2,1,0:T(8,128)}, u32[]{:S(2)}, u32[]{:S(2)}) collective-permute-start(f32[3,16,4096]{2,1,0:T(8,128)} %constant_dynamic-slice_fusion), channel_id=1, source_target_pairs={{4,0},{8,4},{12,8},{0,12},{5,1},{9,5},{13,9},{1,13},{6,2},{10,6},{... | collective-permute-start | bytes 2359304 | tf_op jit(solution)/shard_map/ppermute | solution.py:488
  20.6 53.8 %collective-permute-start.3 = (f32[3,32,4096]{2,1,0:T(8,128)S(1)}, f32[3,32,4096]{2,1,0:T(8,128)}, u32[]{:S(2)}, u32[]{:S(2)}) collective-permute-start(f32[3,32,4096]{2,1,0:T(8,128)S(1)} %bitcast.26), channel_id=1, source_target_pairs={{0,12},{4,0},{8,4},{12,8},{1,5},{5,9},{9,13},{13,1},{2,14},{6,2},{... | collective-permute-start | bytes 4718600 | tf_op jit(solution)/shard_map/ppermute | solution.py:486
  27.4 1.0 copy-start.7
  32.4 7.3 %collective-permute-start.1 = (f32[11,96,96]{2,1,0:T(8,128)}, f32[11,96,96]{2,1,0:T(8,128)}, u32[]{:S(2)}, u32[]{:S(2)}) collective-permute-start(f32[11,96,96]{2,1,0:T(8,128)} %collective-permute-done.refs_1_), channel_id=1, source_target_pairs={{0,1},{1,0},{2,3},{3,2},{4,5},{5,4},{6,7},{7,6},{8,9},{9,8},{10,11... | collective-permute-start | bytes 1216520 | tf_op jit(solution)/shard_map/ppermute | solution.py:491
  36.1 1.0 copy-start.3
  37.1 2.6 %copy-start.5 = (bf16[2,128,288]{2,1,0:T(8,128)(2,1)S(1)}, bf16[2,128,288]{2,1,0:T(8,128)(2,1)}, u32[]{:S(2)}) copy-start(bf16[2,128,288]{2,1,0:T(8,128)(2,1)} %constant.66.clone.refs_7_.refs_4_) | copy-start | bytes 442372
  37.1 2.6 %copy-start.6 = (bf16[2,128,288]{2,1,0:T(8,128)(2,1)S(1)}, bf16[2,128,288]{2,1,0:T(8,128)(2,1)}, u32[]{:S(2)}) copy-start(bf16[2,128,288]{2,1,0:T(8,128)(2,1)} %constant.67.clone.refs_8_.refs_5_) | copy-start | bytes 442372
  37.1 2.6 %copy-start.10 = (f32[22,96,96]{2,1,0:T(8,128)S(1)}, f32[22,96,96]{2,1,0:T(8,128)}, u32[]{:S(2)}) copy-start(f32[22,96,96]{2,1,0:T(8,128)} %copy-done.9) | copy-start | bytes 2433028
  39.7 26.8 %copy-start.4 = (f32[22,96,96]{2,1,0:T(8,128)S(1)}, f32[22,96,96]{2,1,0:T(8,128)}, u32[]{:S(2)}) copy-start(f32[22,96,96]{2,1,0:T(8,128)} %copy-done.3) | copy-start | bytes 2433028
  39.7 26.8 %copy-start.8 = (f32[22,96,96]{2,1,0:T(8,128)S(1)}, f32[22,96,96]{2,1,0:T(8,128)}, u32[]{:S(2)}) copy-start(f32[22,96,96]{2,1,0:T(8,128)} %copy-done.7) | copy-start | bytes 2433028
  65.8 16.2 %collective-permute-start.2 = (f32[12,48,256]{2,1,0:T(8,128)S(1)}, f32[12,48,256]{2,1,0:T(8,128)S(1)}, u32[]{:S(2)}, u32[]{:S(2)}) collective-permute-start(f32[12,48,256]{2,1,0:T(8,128)S(1)} %get-tuple-element.25), channel_id=1, source_target_pairs={{0,2},{2,0},{1,3},{3,1},{4,6},{6,4},{5,7},{7,5},{8,10},{10,8},{9,1... | collective-permute-start | bytes 1769480 | tf_op jit(solution)/shard_map/ppermute | solution.py:515
  74.3 7.8 %copy-start.11 = (bf16[2,2,2,384,96]{4,3,2,1,0:T(8,128)(2,1)S(1)}, bf16[2,2,2,384,96]{4,3,2,1,0:T(8,128)(2,1)}, u32[]{:S(2)}) copy-start(bf16[2,2,2,384,96]{4,3,2,1,0:T(8,128)(2,1)} %constant.65.clone) | copy-start | bytes 1769476
  74.4 31.5 %collective-permute-start.6 = (f32[23,48,256]{2,1,0:T(8,128)S(1)}, f32[23,48,256]{2,1,0:T(8,128)S(1)}, u32[]{:S(2)}, u32[]{:S(2)}) collective-permute-start(f32[23,48,256]{2,1,0:T(8,128)S(1)} %shard_map.126.refs_0_), channel_id=1, source_target_pairs={{0,2},{2,0},{1,3},{3,1},{4,6},{6,4},{5,7},{7,5},{8,10},{10,8},{9,1... | collective-permute-start | bytes 3391496 | tf_op jit(solution)/shard_map/ppermute | solution.py:515
  82.1 2.1 %collective-permute-start.5 = (f32[12,48,256]{2,1,0:T(8,128)S(1)}, f32[12,48,256]{2,1,0:T(8,128)S(1)}, u32[]{:S(2)}, u32[]{:S(2)}) collective-permute-start(f32[12,48,256]{2,1,0:T(8,128)S(1)} %add.37.refs_0_), channel_id=1, source_target_pairs={{0,1},{1,0},{2,3},{3,2},{4,5},{5,4},{6,7},{7,6},{8,9},{9,8},{10,11... | collective-permute-start | bytes 1769480 | tf_op jit(solution)/shard_map/ppermute | solution.py:523
where the time goes:
time: 117 us
  Pallas kernels  68.4 us (58%)
  waiting for transfers between devices  18.2 us (16%)
  local copies, waits for them, and re-layouts  11 us (9%)
  starting transfers between devices  9.23 us (8%)
  between operations  6.98 us (6%)
  other arithmetic  3.35 us (3%)
    pallas_call x7, Pallas kernels, call(): pl.pallas_call(kernel, out_shape=out_shape, in_specs=[pl.BlockSpec(memory...  68.4 us
    ppermute x2, waiting for transfers between devices, body(): swap = lambda v: lax.ppermute(v, 'slab', [(0, 1), (1, 0)])  17.7 us
    unnamed x24, local copies, waits for them, and re-layouts  4.39 us
    ppermute x1, starting transfers between devices, body(): lax.ppermute(base_half, 'seg', [((s + 1) % segs, s) for s in range(segs)])  3.6 us
    ppermute x1, starting transfers between devices, body(): other = lax.ppermute(share, 'slab', [(0, 1), (1, 0)])  2.93 us
    squeeze x2, local copies, waits for them, and re-layouts, body(): lax.dynamic_slice(t, (which[0], slab) + (0,) * (t.ndim - 2), (1, 1) + t.s...  2.91 us
  transfers between devices with their start and end apart: 7, of which 3 were waited for; matrix products, arithmetic and copies ran while one was open for 7% of the time, Pallas kernels for 45%

commit v1 on v0

--- a/solution.py
+++ b/solution.py
@@ -532,9 +532,566 @@
     return base_gap[None], state_gap[None, None]
 
 
+LANES = 128
+QK = 24
+SIDE_QUADS = 3
+STATE_QUADS = 6
+
+
+def lane_pad(values, axis, size=LANES):
+    pad = [(0, 0)] * values.ndim
+    pad[axis] = (0, size - values.shape[axis])
+    return np.pad(values, pad)
+
+
+def halves(values):
+    values = np.asarray(values, np.float32)
+    high = values.astype(ml_dtypes.bfloat16)
+    return high, (values - high.astype(np.float32)).astype(ml_dtypes.bfloat16)
+
+
+def filter_tables(slabs):
+    rows = N // slabs
+    x = np.arange(N)
+    out = []
+    for cut in cuts():
+        n = np.arange(-cut, cut + 1)
+        d = np.mod(x[:, None] - x[None, :], N)
+        phase = 2 * np.pi / N * n[:, None, None] * -d
+        plain = np.cos(phase).sum(0) / N
+        deriv = (-n[:, None, None] * np.sin(phase)).sum(0) / N
+        both_kinds = np.stack([plain, deriv]).reshape(2, slabs, rows, slabs, rows)
+        per_slab = []
+        for slab in range(slabs):
+            blocks = []
+            for source in (slab, 1 - slab):
+                wide = np.zeros((3, rows, 2, LANES))
+                for i in range(3):
+                    wide[i, :, :, i * rows : (i + 1) * rows] = both_kinds[
+                        :, source, :, slab
+                    ].transpose(1, 0, 2)
+                blocks.append(halves(lane_pad(wide.reshape(3 * rows, 2 * LANES), 0)))
+            (own_high, own_low), (far_high, far_low) = blocks
+            per_slab.append(
+                np.concatenate([own_high, own_high, far_high, far_high, own_low, far_low])
+            )
+        out.append(np.stack(per_slab))
+    return np.stack(out, axis=1)
+
+
+def ahead_tables(slabs):
+    rows = N // slabs
+    n = signed()
+    count = len(n)
+    a = angles(np.arange(N), n).reshape(slabs, rows, count)
+    c, s = np.cos(a), np.sin(a)
+    w = np.zeros((slabs, 2, 2, 3, rows, 3, 2, 64))
+    for i in range(3):
+        w[:, 0, 0, i, :, i, 0, :count] = c
+        w[:, 0, 0, i, :, i, 1, :count] = -s
+        w[:, 0, 1, i, :, i, 0, :count] = s
+        w[:, 0, 1, i, :, i, 1, :count] = c
+    w[:, 1, :, :, :, :, 0, :count] = -n * w[:, 0, :, :, :, :, 1, :count]
+    w[:, 1, :, :, :, :, 1, :count] = n * w[:, 0, :, :, :, :, 0, :count]
+    high, low = halves(lane_pad(w.reshape(slabs, 2, 2, 3 * rows, 3 * LANES), 3))
+    blocks = []
+    for kind in range(2):
+        h, l = high[:, kind], low[:, kind]
+        blocks += [h[:, 0], h[:, 0], h[:, 1], h[:, 1], l[:, 0], l[:, 1]]
+    return np.concatenate(blocks, axis=1)
+
+
+def behind_tables(parts):
+    rows = N // parts
+    n = signed()
+    count = len(n)
+    a = angles(n, np.arange(N)).reshape(count, parts, rows).transpose(1, 0, 2)
+    c, s = np.cos(a) / N, np.sin(a) / N
+    w = np.zeros((parts, 3, 2, 64, 2, LANES))
+    for i in range(3):
+        place = slice(i * rows, (i + 1) * rows)
+        w[:, i, 0, :count, 0, place] = c
+        w[:, i, 1, :count, 0, place] = -s
+        w[:, i, 0, :count, 1, place] = s
+        w[:, i, 1, :count, 1, place] = c
+    high, low = halves(w.reshape(parts, 3 * LANES, 2 * LANES))
+    return np.concatenate([high, high, low], axis=1)
+
+
+def force_table():
+    wave = np.arange(1, 5)
+    phase = np.mod(np.outer(wave, np.arange(N)), N).astype(np.float32) * np.float32(2 * np.pi / N)
+    return np.repeat(np.float32(forcing_amp) * np.sin(phase), N, axis=1)[:, None].astype(np.float32)
+
+
+def cat(values, axis):
+    return jnp.concatenate(values, axis=axis)
+
+
+def wide_rows(*fields):
+    blank = jnp.zeros((LANES - fields[0].shape[0], LANES), f32)
+    return cat([part for field in fields for part in (field, blank)], 0)
+
+
+def matmul(left, right):
+    return lax.dot_general(left, right, NN, preferred_element_type=f32)
+
+
+def half_lane(shape):
+    return lax.rem(lax.broadcasted_iota(jnp.int32, shape, 1), 64)
+
+
+def turn(value, shift):
+    return pltpu.roll(value, shift % LANES, 1)
+
+
+GAP = 2 * THIRD + 1
+STEP = 64 - GAP
+PIECES = (GAP, GAP - STEP, GAP - 2 * STEP)
+
+
+def pack_pair(first, second):
+    gap = half_lane(first[0].shape) >= GAP
+    carried = (first[0], second[0], first[1])
+    return [jnp.where(gap, turn(second[1], by), held) for by, held in zip(PIECES, carried)]
+
+
+def unpack_pair(tiles):
+    lane = half_lane(tiles[0].shape)
+    last = turn(tiles[2], -PIECES[2])
+    last = jnp.where(lane < 2 * STEP, turn(tiles[1], -PIECES[1]), last)
+    last = jnp.where(lane < STEP, turn(tiles[0], -PIECES[0]), last)
+    return (tiles[0], tiles[2]), (tiles[1], last)
+
+
+def pack_share(planes):
+    lane = lax.broadcasted_iota(jnp.int32, planes[0].shape, 1)
+    return [jnp.where(lane < 96, planes[i], turn(planes[3], 96 - 32 * i)) for i in range(3)]
+
+
+def unpack_share(tiles):
+    lane = lax.broadcasted_iota(jnp.int32, tiles[0].shape, 1)
+    last = jnp.where(lane < 64, turn(tiles[1], 64), turn(tiles[2], 96))
+    return [*tiles, jnp.where(lane < 32, turn(tiles[0], 32), last)]
+
+
+def two_columns(work, k):
+    return cat([work[column(k), :], work[column(k + 1), :]], 1)
+
+
+def fused(
+    base_hbm, state_hbm, cutoff_ref, wave_ref, wz_hbm, wy_hbm, pd_hbm, xt_hbm, xs_hbm, xb_hbm,
+    yb_hbm, zb_hbm, force_hbm, base_gap_hbm, state_gap_hbm,
+    base_v, state_v, near_base, near_state, wz, wy, pd, xt, xs, xb, yb, zb, force,
+    w0, w1, w2, wa, wb, wc, own, share, other, partner, g, f,
+    base_send, base_recv, base_sum, state_send, state_recv, out_base, out_state,
+    local_sem, out_sem, near_send, near_recv, share_send, share_recv, pass_send, pass_recv,
+    base_send_sem, base_recv_sem, sum_send, sum_recv, state_send_sem, state_recv_sem,
+):
+    side = lax.axis_index("comp")
+    slab = lax.axis_index("slab")
+    seg = lax.axis_index("seg")
+    segs = lax.axis_size("seg")
+    far = {"slab": 1 - slab}
+    twin = {"comp": 1 - side}
+    after, before = lax.rem(seg + 1, segs), lax.rem(seg + segs - 1, segs)
+    half = near_base.shape[1]
+    quarter = N * N // 4
+
+    def local(index, src, dst):
+        return pltpu.make_async_copy(src, dst, local_sem.at[index])
+
+    def remote(src, dst, send, recv, device):
+        return pltpu.make_async_remote_copy(
+            src_ref=src, dst_ref=dst, send_sem=send, recv_sem=recv, device_id=device,
+            device_id_type=pl.DeviceIdType.MESH,
+        )
+
+    barrier = pltpu.get_barrier_semaphore()
+    for device in (far, twin, {"seg": after}, {"seg": before}):
+        pl.semaphore_signal(
+            barrier, inc=1, device_id=device, device_id_type=pl.DeviceIdType.MESH
+        )
+
+    def quarter_of(ref, i):
+        return ref.at[:, :, pl.ds(i * quarter, quarter)]
+
+    wz_copy = local(0, wz_hbm, wz)
+    base_copies = [
+        local(1 + i, quarter_of(base_hbm, i), quarter_of(base_v, i)) for i in range(4)
+    ]
+    wy_copy = local(5, wy_hbm, wy)
+    state_copy = local(6, state_hbm, state_v)
+    late_copies = [
+        local(7, pd_hbm.at[slab], pd),
+        local(8, yb_hbm, yb),
+        local(9, zb_hbm, zb),
+        local(10, force_hbm, force),
+        local(11, xt_hbm.at[slab], xt),
+        local(12, xs_hbm.at[slab], xs),
+        local(13, xb_hbm.at[2 * slab + side], xb),
+    ]
+    for copy in (wz_copy, *base_copies, wy_copy, state_copy, *late_copies):
+        copy.start()
+
+    pl.semaphore_wait(barrier, 4)
+    near_copies = [
+        remote(
+            state_hbm, near_state, near_send.at[0], near_recv.at[0],
+            {"seg": jnp.where(side == 0, before, after)},
+        ),
+        remote(
+            base_hbm.at[:, pl.ds(half * side, half), :], near_base, near_send.at[1],
+            near_recv.at[1], {"seg": before},
+        ),
+    ]
+    for copy in near_copies:
+        copy.start()
+
+    cut_x, cut_y, cut_z = (cutoff_ref[i] for i in range(3))
+    at_x, at_y, at_z = (jnp.clip(cut - LOW, 0, THIRD - LOW) for cut in (cut_x, cut_y, cut_z))
+
+    def base_ahead_z(p):
+        w0[pair_rows(p), :] = left3(wz[at_z, 0], wide_rows(flat(base_v[:, :, lanes(p)])), NT)
+
+    wz_copy.wait()
+    for i, copy in enumerate(base_copies):
+        copy.wait()
+        loop(PAIRS // 4, Z1, lambda p, i=i: base_ahead_z(p + i * (PAIRS // 4)))
+    wy_copy.wait()
+
+    def base_planes(q):
+        planes = []
+        for j in (0, 2):
+            both_planes = left3(wy[at_y, 0], two_columns(w0, 4 * q + j), NN)
+            planes += [both_planes[:, :LANES], both_planes[:, LANES:]]
+        for i in range(4):
+            own[4 * q + i] = planes[i]
+        return planes
+
+    share_copies = []
+    for t in range(SIDE_QUADS):
+        for i, tile in enumerate(pack_share(base_planes(SIDE_QUADS * side + t))):
+            share[3 * t + i] = tile
+        rows = pl.ds(3 * t, 3)
+        copy = remote(
+            share.at[rows], other.at[rows], share_send.at[t], share_recv.at[t], far
+        )
+        copy.start()
+        share_copies.append(copy)
+    for t in range(SIDE_QUADS):
+        base_planes(SIDE_QUADS * (1 - side) + t)
+
+    pass_copies = []
+
+    def pass_on(t):
+        share_copies[t].wait_recv()
+        rows = pl.ds(3 * t, 3)
+        copy = remote(
+            other.at[rows], partner.at[rows], pass_send.at[t], pass_recv.at[t], twin
+        )
+        copy.start()
+        pass_copies.append(copy)
+
+    state_copy.wait()
+    scale = sign_step()
+
+    def flux_z(t):
+        first, second = [], []
+        for i in range(2):
+            p = 2 * t + i
+            state = state_v[:, :, lanes(p)]
+            scaled = state * scale
+            f0, f1, f2 = (flat(scaled * base_v[j, :, lanes(p)][None]) for j in range(3))
+            plain = left3(wz[at_z, 0], wide_rows(flat(state), f0), NT)
+            wa[pair_rows(p), :] = plain[:, :LANES]
+            wc[pair_rows(p), :] = plain[:, LANES:]
+            first.append(f1)
+            second.append(f2)
+        along_y = left3(wz[at_z, 0], wide_rows(*first), NT)
+        along_z = left3(wz[at_z, 1], wide_rows(*second), NT)
+        for i in range(2):
+            p = 2 * t + i
+            mine = slice(i * LANES, (i + 1) * LANES)
+            wb[pair_rows(p), :] = along_y[:, mine]
+            wa[pair_rows(p), :] += along_z[:, mine]
+
+    loop(PAIRS // 2, 2, flux_z)
+    pass_on(0)
+
+    def flux_y(t):
+        k = 2 * t
+        extra = left3(wy[at_y, 1], two_columns(wb, k), NN)
+        for i in range(2):
+            whole = left3(
+                wy[at_y, 0], cat([wa[column(k + i), :], wc[column(k + i), :]], 1), NN
+            )
+            g[k + i] = whole[:, :LANES] + extra[:, i * LANES : (i + 1) * LANES]
+            f[k + i] = whole[:, LANES:]
+
+    loop(QK // 2, 2, flux_y)
+    pass_on(1)
+
+    for copy in late_copies:
+        copy.wait()
+
+    def back_y(ref, place, t):
+        q = SIDE_QUADS * place + t
+        planes = unpack_share([ref[3 * t + i] for i in range(3)])
+        deep = []
+        for i in range(4):
+            own_high, own_low = split(own[4 * q + i])
+            far_high, far_low = split(planes[i])
+            deep.append(cat([own_high, own_low, far_high, far_low, own_high, far_high], 1))
+        filtered = matmul(cat(deep, 0), pd[at_x])
+        kinds = [filtered[96 * i : 96 * (i + 1)] for i in range(4)]
+        for j in (0, 2):
+            along = left3(yb[1], cat([kinds[j][:, :LANES], kinds[j + 1][:, :LANES]], 1), NN)
+            for i in range(2):
+                k = 4 * q + j + i
+                whole = left3(yb[0], kinds[j + i], NN)
+                w2[column(k), :] = whole[:, :LANES]
+                w0[column(k), :] = whole[:, LANES:]
+                w1[column(k), :] = along[:, i * LANES : (i + 1) * LANES]
+
+    back_y(other, side, 0)
+    back_y(other, side, 1)
+    pass_on(2)
+    back_y(other, side, 2)
+    for t in range(SIDE_QUADS):
+        pass_copies[t].wait_recv()
+        back_y(partner, 1 - side, t)
+
+    tangent = side == 0
+    wave = jnp.clip(wave_ref[0] - 1, 0, 3)
+
+    def grid_space(t):
+        third = left3(
+            zb[1], cat([w2[pair_rows(2 * t + i), :] for i in range(2)], 1), NN
+        ).T
+        for i in range(2):
+            p = 2 * t + i
+            state = state_v[:, :, lanes(p)]
+            base = base_v[:, :, lanes(p)]
+            pair = left3(zb[0], cat([w0[pair_rows(p), :], w1[pair_rows(p), :]], 1), NN).T
+            grad = [
+                pair[:96].reshape(base.shape),
+                pair[LANES : LANES + 96].reshape(base.shape),
+                third[i * LANES : i * LANES + 96].reshape(base.shape),
+            ]
+            coupled, driven = [], []
+            for a in range(3):
+                total = 0.0
+                drive = 0.0
+                for b in range(3):
+                    total = total + jnp.where(tangent, grad[b][a], grad[a][b]) * state[b]
+                    drive = drive + grad[b][a] * base[b]
+                if a == 0:
+                    drive = drive - force[wave, :, lanes(p)]
+                coupled.append(-time_step * total)
+                driven.append(base[a] - time_step * drive)
+            out = left3(wz[at_z, 0], wide_rows(cat(coupled, 0), cat(driven, 0)), NT)
+            wa[pair_rows(p), :] = out[:, :LANES]
+            wb[pair_rows(p), :] = out[:, LANES:]
+
+    loop(PAIRS // 2, 2, grid_space)
+
+    waves = plane_waves()
+    keep = jnp.where(jnp.abs(waves[0]) <= cut_x.astype(f32), 1.0, 0.0)
+
+    def ahead_deep(plane):
+        high, low = split(plane)
+        return [high[:MP], low[:MP], high[MP:], low[MP:], high[:MP], high[MP:]]
+
+    def emit_planes(ref, first_tile, first_k, modes, count, third):
+        new = []
+        for i in range(count):
+            w = projected(waves, modes[MP * i : MP * (i + 1)], first_k + i)
+            new.append([keep * part for part in w])
+        if third:
+            ref[0] = new[0][2]
+        for j in range(0, count, 2):
+            for i, tile in enumerate(pack_pair(new[j], new[j + 1])):
+                ref[first_tile + 3 * (j // 2) + i] = tile
+
+    def quad_tiles(q, pairs=2):
+        return pl.ds(0, 7) if q == 0 else pl.ds(1 + 6 * q, 3 * pairs)
+
+    base_copies = []
+    for t in range(SIDE_QUADS):
+        q = SIDE_QUADS * side + t
+        deep = []
+        for j in (0, 2):
+            both_planes = left3(wy[at_y, 0], two_columns(wb, 4 * q + j), NN)
+            for i in range(2):
+                deep.append(cat(ahead_deep(both_planes[:, i * LANES : (i + 1) * LANES]), 1))
+        modes = matmul(cat(deep, 0), xt[: 6 * LANES])
+        emit_planes(base_send, 1 + 6 * t, 4 * q, modes, 4, t == 0)
+        rows = quad_tiles(t)
+        copy = remote(
+            base_send.at[rows], base_recv.at[rows], base_send_sem.at[t], base_recv_sem.at[t],
+            far,
+        )
+        copy.start()
+        base_copies.append(copy)
+
+    state_copies = []
+    for q in range(STATE_QUADS):
+        pairs = 2 if q < STATE_QUADS - 1 else 1
+        deep = []
+        for j in range(0, 2 * pairs, 2):
+            both_planes = left3(wy[at_y, 0], two_columns(wa, 4 * q + j), NN)
+            for i in range(2):
+                k = 4 * q + j + i
+                total = g[k] + both_planes[:, i * LANES : (i + 1) * LANES]
+                deep.append(cat(ahead_deep(total) + ahead_deep(f[k]), 1))
+        modes = matmul(cat(deep, 0), xt[...])
+        emit_planes(state_send, 1 + 6 * q, 4 * q, modes, 2 * pairs, q == 0)
+        rows = quad_tiles(q, pairs)
+        copy = remote(
+            state_send.at[rows], state_recv.at[rows], state_send_sem.at[q],
+            state_recv_sem.at[q], far,
+        )
+        copy.start()
+        state_copies.append(copy)
+
+    def spectral(tiles, third, first_k, table_ref, work):
+        deep = []
+        wave_x, wave_y = waves
+        for j in range(len(tiles) // 3):
+            for i, (m0, m1) in enumerate(unpack_pair(tiles[3 * j : 3 * j + 3])):
+                k = jnp.asarray(first_k + 2 * j + i, jnp.int32)
+                inverse = 1.0 / jnp.maximum(k, 1).astype(f32)
+                m2 = -(wave_x * m0 + wave_y * m1) * inverse
+                if third is not None and j == 0 and i == 0:
+                    m2 = jnp.where(k == 0, third, m2)
+                high, low = split(cat([m0, m1, m2], 1))
+                deep.append(cat([high, low, high], 1))
+        rows = matmul(cat(deep, 0), table_ref[...])
+        planes = []
+        for i in range(len(deep)):
+            mine = rows[MP * i : MP * (i + 1)]
+            planes.append(cat([mine[:, :LANES], mine[:, LANES:]], 0))
+        for j in range(0, len(deep), 2):
+            out = left3(yb[0], cat(planes[j : j + 2], 1), NN)
+            for i in range(2):
+                work[column(first_k + j + i), :] = out[:, i * LANES : (i + 1) * LANES]
+
+    span = base_sum.shape[0] // 2
+    sum_copies = []
+    for t in range(SIDE_QUADS):
+        base_copies[t].wait_recv()
+        for i in range(7 if t == 0 else 6):
+            tile = i if t == 0 else 1 + 6 * t + i
+            base_sum[span * side + tile] = base_send[tile] + base_recv[tile]
+        start = 0 if t == 0 else 1 + 6 * t
+        rows = pl.ds(span * side + start, 7 if t == 0 else 6)
+        copy = remote(
+            base_sum.at[rows], base_sum.at[rows], sum_send.at[t], sum_recv.at[t], twin
+        )
+        copy.start()
+        sum_copies.append(copy)
+
+    def base_back(place, t):
+        first = span * place
+        tiles = [base_sum[first + 1 + 6 * t + i] for i in range(6)]
+        third = base_sum[first] if t == 0 else None
+        spectral(tiles, third, 4 * (SIDE_QUADS * place + t), xb, w0)
+
+    for t in range(SIDE_QUADS):
+        base_back(side, t)
+    for t in range(SIDE_QUADS):
+        sum_copies[t].wait_recv()
+        base_back(1 - side, t)
+
+    for q in range(STATE_QUADS):
+        state_copies[q].wait_recv()
+        count = 6 if q < STATE_QUADS - 1 else 3
+        both_tiles = lambda tile: state_send[tile] + state_recv[tile]
+        tiles = [both_tiles(1 + 6 * q + i) for i in range(count)]
+        spectral(tiles, both_tiles(0) if q == 0 else None, 4 * q, xs, wc)
+
+    for copy in near_copies:
+        copy.wait_recv()
+
+    def finish_z(p):
+        rows = left3(zb[0], cat([wc[pair_rows(p), :], w0[pair_rows(p), :]], 1), NN).T
+        near = near_state[:, :, lanes(p)]
+        out_state[:, :, lanes(p)] = rows[:96].reshape(near.shape) - near
+        near = near_base[:, :, lanes(p)]
+        out_base[:, :, lanes(p)] = rows[LANES : LANES + 48].reshape(near.shape) - near
+
+    out_copies = []
+    for i in range(4):
+        loop(PAIRS // 4, 4, lambda p, i=i: finish_z(p + i * (PAIRS // 4)))
+        for j, (src, dst) in enumerate(((out_state, state_gap_hbm), (out_base, base_gap_hbm))):
+            copy = pltpu.make_async_copy(
+                quarter_of(src, i), quarter_of(dst, i), out_sem.at[2 * i + j]
+            )
+            copy.start()
+            out_copies.append(copy)
+
+    sent = near_copies + share_copies + pass_copies + base_copies + sum_copies + state_copies
+    for copy in sent:
+        copy.wait_send()
+    for copy in out_copies:
+        copy.wait()
+
+
+def fused_body(base, state, wavenumber, cutoff):
+    base, state = base[0], state[0, 0]
+    rows = base.shape[1]
+    half = rows // lax.axis_size("comp")
+    slabs = lax.axis_size("slab")
+    tables = [
+        z_tables(), y_tables(), filter_tables(slabs), ahead_tables(slabs), behind_tables(slabs),
+        behind_tables(2 * slabs), y_back(), z_back(), force_table(),
+    ]
+    tables = [jnp.asarray(t) for t in tables]
+    hbm = pl.BlockSpec(memory_space=pltpu.HBM)
+    smem = pl.BlockSpec(memory_space=pltpu.SMEM)
+    vmem = lambda *shape: pltpu.VMEM(shape, f32)
+    dma = lambda count: pltpu.SemaphoreType.DMA((count,))
+    held = lambda t: pltpu.VMEM(t.shape, t.dtype)
+    held_one = lambda t: pltpu.VMEM(t.shape[1:], t.dtype)
+    wz, wy, pd, xt, xs, xb, yb, zb, force = tables
+    work = vmem(2 * N * KP, LANES)
+    share = vmem(3 * SIDE_QUADS, 2 * MP, LANES)
+    planes = vmem(QK, 2 * MP, LANES)
+    base_tiles = vmem(1 + 6 * SIDE_QUADS, MP, LANES)
+    state_tiles = vmem(4 + 6 * (STATE_QUADS - 1), MP, LANES)
+    base_half = vmem(3, half, N * N)
+    whole = vmem(3, rows, N * N)
+    scratch = [
+        whole, whole, base_half, whole, held(wz), held(wy), held_one(pd), held_one(xt),
+        held_one(xs), held_one(xb), held(yb), held(zb), held(force),
+        *[work] * 6, planes, share, share, share, planes, planes,
+        base_tiles, base_tiles, vmem(2 + 12 * SIDE_QUADS, MP, LANES), state_tiles, state_tiles,
+        base_half, whole,
+        dma(14), dma(8), dma(2), dma(2), *[dma(SIDE_QUADS)] * 8, *[dma(STATE_QUADS)] * 2,
+    ]
+    base_gap, state_gap = pl.pallas_call(
+        fused,
+        out_shape=(
+            jax.ShapeDtypeStruct((3, half, N * N), f32),
+            jax.ShapeDtypeStruct((3, rows, N * N), f32),
+        ),
+        in_specs=[hbm, hbm, smem, smem, *[hbm] * len(tables)],
+        out_specs=(hbm, hbm),
+        scratch_shapes=scratch,
+        compiler_params=pltpu.CompilerParams(
+            vmem_limit_bytes=56 * 2**20, collective_id=0, has_side_effects=True
+        ),
+        cost_estimate=pl.CostEstimate(flops=10**10, bytes_accessed=10**7, transcendentals=0),
+    )(base, state, cutoff, wavenumber, *tables)
+    return base_gap[None], state_gap[None, None]
+
+
 def solution(mesh):
+    sizes = dict(mesh.shape)
+    one_kernel = sizes["slab"] == 2 and sizes["comp"] == 2 and sizes["seg"] > 1
     return jax.shard_map(
-        body,
+        fused_body if one_kernel else body,
         mesh=mesh,
         in_specs=(
             P(("groups", "seg"), None, "slab", None),

time: 117 us -> 72.7 us (0.62)
  waiting for transfers between devices: 18.2 us -> 0 us
  starting transfers between devices: 9.23 us -> 0 us
  local copies, waits for them, and re-layouts: 11 us -> 3.33 us
  between operations: 6.98 us -> 1.29 us
  other arithmetic: 3.35 us -> 0 us
    ppermute x7 -> x0, waiting for transfers between devices: 18.2 us -> none  [the longest x2 17.7 us: body(): swap = lambda v: lax.ppermute(v, 'slab', [(0, 1), (1, 0)])]
    ppermute x7 -> x0, starting transfers between devices: 9.23 us -> none  [the longest x1 3.6 us: body(): lax.ppermute(base_half, 'seg', [((s + 1) % segs, s) for s in range(segs)])]
    squeeze x4 -> x0, local copies, waits for them, and re-layouts: 3.97 us -> none  [the longest x2 2.91 us: body(): lax.dynamic_slice(t, (which[0], slab) + (0,) * (t.ndim - 2), (1, 1) + t.s...]
    concatenate x1 -> x0, other arithmetic: 1.48 us -> none  [body(): near_wide = jnp.concatenate([near_base, near_base], axis=1)]
    unnamed x24 -> x4, local copies, waits for them, and re-layouts: 4.39 us -> 3.33 us
    pallas_call x7 -> x1, Pallas kernels: 68.4 us -> 67.9 us  [fused_body(): pl.pallas_call(fused, out_shape=(jax.ShapeDtypeStruct((3, half, N * N), f...]
  transfers between devices with their start and end apart: 7 -> 0, of which waited for: 3 -> 0; matrix products, arithmetic and copies ran while one was open for 7% -> 0% of each run, Pallas kernels for 45% -> 0%
where the time goes in v1:
time: 72.7 us; the launch traced here: 72.5 us
  Pallas kernels  67.9 us (93%)
  local copies, waits for them, and re-layouts  3.33 us (5%)
  between operations  1.29 us (2%)
    pallas_call x1, Pallas kernels, fused_body(): pl.pallas_call(fused, out_shape=(jax.ShapeDtypeStruct((3, half, N * N), f...  67.9 us
    unnamed x4, local copies, waits for them, and re-layouts  3.33 us

profile of v1, /device:TPU:0, one launch (start us, length us, event | category | flops | bytes accessed | tf_op | source)
XLA Modules:
  0.0 72.5 jit_solution(17570525001457896198)
XLA Ops:
  1.3 67.9 %shard_map.140 = (f32[3,16,4096]{2,1,0:T(8,128)}, f32[3,32,4096]{2,1,0:T(8,128)}) custom-call(f32[3,32,4096]{2,1,0:T(8,128)} %bitcast.6, f32[3,32,4096]{2,1,0:T(8,128)} %bitcast.7, s32[3]{0:T(128)} %cutoff_ref.1, s32[1]{0:T(128)S(6)} %copy.17.wave_ref, bf16[4,2,96,384]{3,2,1,0:T(8,128)(2,1)} %constant.18.clone.wz_hbm, ...), custom_call_target="tpu_custom_call" | custom-call | flops 10000000000 | bytes 10000000 | tf_op jit(solution)/shard_map/pallas_call | solution.py:1073
  69.2 0.0 copy-start
  69.2 2.2 %copy.18 = f32[1,3,16,4096]{3,2,1,0:T(8,128)} copy(f32[1,3,16,4096]{3,2,1,0:T(8,128)} %bitcast.5) | data formatting | bytes 1572864
  71.4 0.0 copy-done
  71.4 1.1 %copy.19 = f32[1,1,3,32,4096]{4,3,2,1,0:T(8,128)} copy(f32[1,1,3,32,4096]{4,3,2,1,0:T(8,128)S(1)} %bitcast.4) | data formatting | bytes 3145728
Async XLA Ops:
  69.2 2.2 %copy-start = (f32[3,32,4096]{2,1,0:T(8,128)S(1)}, f32[3,32,4096]{2,1,0:T(8,128)}, u32[]{:S(2)}) copy-start(f32[3,32,4096]{2,1,0:T(8,128)} %get-tuple-element.5) | copy-start | bytes 4718596

commit v2 on v1

--- a/solution.py
+++ b/solution.py
@@ -536,6 +536,7 @@
 QK = 24
 SIDE_QUADS = 3
 STATE_QUADS = 6
+FLUX_FIRST = 8
 
 
 def lane_pad(values, axis, size=LANES):
@@ -618,10 +619,36 @@
     return np.concatenate([high, high, low], axis=1)
 
 
-def force_table():
-    wave = np.arange(1, 5)
-    phase = np.mod(np.outer(wave, np.arange(N)), N).astype(np.float32) * np.float32(2 * np.pi / N)
-    return np.repeat(np.float32(forcing_amp) * np.sin(phase), N, axis=1)[:, None].astype(np.float32)
+def table_groups():
+    blocks = lambda t, height: t.reshape(-1, height, t.shape[-1])
+    wide = [z_tables(), y_tables()]
+    wide += [lane_pad(lane_pad(t, 1, 4 * MP), 2, 3 * LANES) for t in (y_back(), z_back())]
+    wide.append(ahead_tables(2))
+    narrow = [filter_tables(2), behind_tables(2), behind_tables(4)]
+    return [blocks(t, 2 * MP) for t in wide], [blocks(t, 3 * LANES) for t in narrow]
+
+
+def table_places():
+    counts = (1, 1, 1, 1, 2), (2, 2, 4)
+    places = []
+    for group, shares in zip(table_groups(), counts):
+        start, entries = 0, []
+        for t, share in zip(group, shares):
+            entries.append((start, len(t) // share))
+            start += len(t)
+        places.append(entries)
+    return places
+
+
+def quarter_sine(position):
+    folded = lax.rem(position, N // 2)
+    folded = jnp.minimum(folded, N // 2 - folded)
+    angle = folded.astype(f32) * (2.0 * np.pi / N)
+    square = angle * angle
+    series = 1.0
+    for order in (12, 10, 8, 6, 4, 2):
+        series = 1.0 - series * square * (1.0 / (order * (order + 1)))
+    return jnp.where(position < N // 2, 1.0, -1.0) * angle * series
 
 
 def cat(values, axis):
@@ -648,6 +675,9 @@
 GAP = 2 * THIRD + 1
 STEP = 64 - GAP
 PIECES = (GAP, GAP - STEP, GAP - 2 * STEP)
+BODY = 40
+PAIR_ROWS = 3 * BODY + 16
+QUAD_ROWS = PAIR_ROWS + 3 * BODY + 8
 
 
 def pack_pair(first, second):
@@ -664,12 +694,54 @@
     return (tiles[0], tiles[2]), (tiles[1], last)
 
 
+def tails(first, second):
+    low = lax.broadcasted_iota(jnp.int32, first.shape, 0) < 4
+    return jnp.where(low, first, pltpu.roll(second, 4, 0))
+
+
+def squeeze(tile):
+    return cat([tile[:BODY], tile[MP : MP + BODY], tails(tile[BODY:MP], tile[MP + BODY :])], 0)
+
+
+def unsqueeze(held):
+    tail = held[2 * BODY :]
+    return cat([held[:BODY], tail, held[BODY : 2 * BODY], pltpu.roll(tail, 4, 0)], 0)
+
+
+def pack_quad(tiles):
+    body = [tile[:BODY] for tile in tiles]
+    tail = [tile[BODY:] for tile in tiles]
+    if len(tiles) == 3:
+        return cat([*body, tails(tail[0], tail[1]), tail[2]], 0)
+    return cat(
+        [
+            *body[:3], tails(tail[0], tail[1]), tails(tail[2], tail[5]),
+            *body[3:], tails(tail[3], tail[4]),
+        ],
+        0,
+    )
+
+
+def unpack_quad(held):
+    part = lambda start, size: held[start : start + size]
+    body = [part(BODY * i, BODY) for i in range(3)]
+    first, second = part(3 * BODY, 8), part(3 * BODY + 8, 8)
+    tail = [first, pltpu.roll(first, 4, 0), second]
+    if held.shape[0] > PAIR_ROWS:
+        body += [part(PAIR_ROWS + BODY * i, BODY) for i in range(3)]
+        last = part(PAIR_ROWS + 3 * BODY, 8)
+        tail += [last, pltpu.roll(last, 4, 0), pltpu.roll(second, 4, 0)]
+    return [cat([b, t], 0) for b, t in zip(body, tail)]
+
+
 def pack_share(planes):
     lane = lax.broadcasted_iota(jnp.int32, planes[0].shape, 1)
-    return [jnp.where(lane < 96, planes[i], turn(planes[3], 96 - 32 * i)) for i in range(3)]
-
-
-def unpack_share(tiles):
+    tiles = [jnp.where(lane < 96, planes[i], turn(planes[3], 96 - 32 * i)) for i in range(3)]
+    return [squeeze(tile) for tile in tiles]
+
+
+def unpack_share(held):
+    tiles = [unsqueeze(part) for part in held]
     lane = lax.broadcasted_iota(jnp.int32, tiles[0].shape, 1)
     last = jnp.where(lane < 64, turn(tiles[1], 64), turn(tiles[2], 96))
     return [*tiles, jnp.where(lane < 32, turn(tiles[0], 32), last)]
@@ -680,12 +752,10 @@
 
 
 def fused(
-    base_hbm, state_hbm, cutoff_ref, wave_ref, wz_hbm, wy_hbm, pd_hbm, xt_hbm, xs_hbm, xb_hbm,
-    yb_hbm, zb_hbm, force_hbm, base_gap_hbm, state_gap_hbm,
-    base_v, state_v, near_base, near_state, wz, wy, pd, xt, xs, xb, yb, zb, force,
-    w0, w1, w2, wa, wb, wc, own, share, other, partner, g, f,
-    base_send, base_recv, base_sum, state_send, state_recv, out_base, out_state,
-    local_sem, out_sem, near_send, near_recv, share_send, share_recv, pass_send, pass_recv,
+    base_hbm, state_hbm, cutoff_ref, wave_ref, wide_hbm, narrow_hbm, out_base, out_state,
+    base_v, state_v, near_base, near_state, wz_v, wy_v, pd_v, xt, xs, xb, yb_v, zb_v,
+    w0, w1, w2, wa, wb, wc, wd, held_coupled, own, share, other, partner, g, f,
+    base_send, base_recv, base_sum, state_send, state_recv, local_sem, near_send, near_recv, share_send, share_recv, pass_send, pass_recv,
     base_send_sem, base_recv_sem, sum_send, sum_recv, state_send_sem, state_recv_sem,
 ):
     side = lax.axis_index("comp")
@@ -716,25 +786,60 @@
     def quarter_of(ref, i):
         return ref.at[:, :, pl.ds(i * quarter, quarter)]
 
-    wz_copy = local(0, wz_hbm, wz)
+    wide_places, narrow_places = table_places()
+
+    def table_part(hbm, entry, index, dst):
+        start, rows = entry
+        return hbm.at[pl.ds(start + rows * index, rows)], dst
+
+    wz_copy = local(0, *table_part(wide_hbm, wide_places[0], 0, wz_v))
     base_copies = [
         local(1 + i, quarter_of(base_hbm, i), quarter_of(base_v, i)) for i in range(4)
     ]
-    wy_copy = local(5, wy_hbm, wy)
+    wy_copy = local(5, *table_part(wide_hbm, wide_places[1], 0, wy_v))
     state_copy = local(6, state_hbm, state_v)
     late_copies = [
-        local(7, pd_hbm.at[slab], pd),
-        local(8, yb_hbm, yb),
-        local(9, zb_hbm, zb),
-        local(10, force_hbm, force),
-        local(11, xt_hbm.at[slab], xt),
-        local(12, xs_hbm.at[slab], xs),
-        local(13, xb_hbm.at[2 * slab + side], xb),
+        local(7, *table_part(narrow_hbm, narrow_places[0], slab, pd_v)),
+        local(8, *table_part(wide_hbm, wide_places[2], 0, yb_v)),
+        local(9, *table_part(wide_hbm, wide_places[3], 0, zb_v)),
+        local(10, *table_part(wide_hbm, wide_places[4], slab, xt)),
+        local(11, *table_part(narrow_hbm, narrow_places[1], slab, xs)),
+        local(12, *table_part(narrow_hbm, narrow_places[2], 2 * slab + side, xb)),
     ]
-    for copy in (wz_copy, *base_copies, wy_copy, state_copy, *late_copies):
+    for copy in (wz_copy, *base_copies, wy_copy, state_copy):
         copy.start()
 
-    pl.semaphore_wait(barrier, 4)
+    cut_x, cut_y, cut_z = (cutoff_ref[i] for i in range(3))
+    at_x, at_y, at_z = (jnp.clip(cut - LOW, 0, THIRD - LOW) for cut in (cut_x, cut_y, cut_z))
+
+    def back_table(ref, kind, depth):
+        return ref[2 * kind : 2 * kind + 2].reshape(4 * MP, 3 * LANES)[: 2 * N, :depth]
+
+    wz = lambda kind: wz_v[2 * at_z + kind]
+    wy = lambda kind: wy_v[2 * at_y + kind]
+    yb = lambda kind: back_table(yb_v, kind, 6 * MP)
+    zb = lambda kind: back_table(zb_v, kind, 12 * KP)
+
+    def base_ahead_z(p):
+        w0[pair_rows(p), :] = left3(wz(0), wide_rows(flat(base_v[:, :, lanes(p)])), NT)
+
+    wz_copy.wait()
+    for i, copy in enumerate(base_copies):
+        copy.wait()
+        loop(PAIRS // 4, Z1, lambda p, i=i: base_ahead_z(p + i * (PAIRS // 4)))
+    for copy in late_copies:
+        copy.start()
+    wy_copy.wait()
+
+    def base_planes(q):
+        planes = []
+        for j in (0, 2):
+            both_planes = left3(wy(0), two_columns(w0, 4 * q + j), NN)
+            planes += [both_planes[:, :LANES], both_planes[:, LANES:]]
+        for i in range(4):
+            own[4 * q + i] = planes[i]
+        return planes
+
     near_copies = [
         remote(
             state_hbm, near_state, near_send.at[0], near_recv.at[0],
@@ -745,34 +850,14 @@
             near_recv.at[1], {"seg": before},
         ),
     ]
-    for copy in near_copies:
-        copy.start()
-
-    cut_x, cut_y, cut_z = (cutoff_ref[i] for i in range(3))
-    at_x, at_y, at_z = (jnp.clip(cut - LOW, 0, THIRD - LOW) for cut in (cut_x, cut_y, cut_z))
-
-    def base_ahead_z(p):
-        w0[pair_rows(p), :] = left3(wz[at_z, 0], wide_rows(flat(base_v[:, :, lanes(p)])), NT)
-
-    wz_copy.wait()
-    for i, copy in enumerate(base_copies):
-        copy.wait()
-        loop(PAIRS // 4, Z1, lambda p, i=i: base_ahead_z(p + i * (PAIRS // 4)))
-    wy_copy.wait()
-
-    def base_planes(q):
-        planes = []
-        for j in (0, 2):
-            both_planes = left3(wy[at_y, 0], two_columns(w0, 4 * q + j), NN)
-            planes += [both_planes[:, :LANES], both_planes[:, LANES:]]
-        for i in range(4):
-            own[4 * q + i] = planes[i]
-        return planes
-
     share_copies = []
     for t in range(SIDE_QUADS):
         for i, tile in enumerate(pack_share(base_planes(SIDE_QUADS * side + t))):
             share[3 * t + i] = tile
+        if t == 0:
+            pl.semaphore_wait(barrier, 4)
+            for copy in near_copies:
+                copy.start()
         rows = pl.ds(3 * t, 3)
         copy = remote(
             share.at[rows], other.at[rows], share_send.at[t], share_recv.at[t], far
@@ -803,34 +888,18 @@
             state = state_v[:, :, lanes(p)]
             scaled = state * scale
             f0, f1, f2 = (flat(scaled * base_v[j, :, lanes(p)][None]) for j in range(3))
-            plain = left3(wz[at_z, 0], wide_rows(flat(state), f0), NT)
+            plain = left3(wz(0), wide_rows(flat(state), f0), NT)
             wa[pair_rows(p), :] = plain[:, :LANES]
             wc[pair_rows(p), :] = plain[:, LANES:]
             first.append(f1)
             second.append(f2)
-        along_y = left3(wz[at_z, 0], wide_rows(*first), NT)
-        along_z = left3(wz[at_z, 1], wide_rows(*second), NT)
+        along_y = left3(wz(0), wide_rows(*first), NT)
+        along_z = left3(wz(1), wide_rows(*second), NT)
         for i in range(2):
             p = 2 * t + i
             mine = slice(i * LANES, (i + 1) * LANES)
             wb[pair_rows(p), :] = along_y[:, mine]
             wa[pair_rows(p), :] += along_z[:, mine]
-
-    loop(PAIRS // 2, 2, flux_z)
-    pass_on(0)
-
-    def flux_y(t):
-        k = 2 * t
-        extra = left3(wy[at_y, 1], two_columns(wb, k), NN)
-        for i in range(2):
-            whole = left3(
-                wy[at_y, 0], cat([wa[column(k + i), :], wc[column(k + i), :]], 1), NN
-            )
-            g[k + i] = whole[:, :LANES] + extra[:, i * LANES : (i + 1) * LANES]
-            f[k + i] = whole[:, LANES:]
-
-    loop(QK // 2, 2, flux_y)
-    pass_on(1)
 
     for copy in late_copies:
         copy.wait()
@@ -843,37 +912,49 @@
             own_high, own_low = split(own[4 * q + i])
             far_high, far_low = split(planes[i])
             deep.append(cat([own_high, own_low, far_high, far_low, own_high, far_high], 1))
-        filtered = matmul(cat(deep, 0), pd[at_x])
+        filtered = matmul(cat(deep, 0), cat([pd_v[2 * at_x], pd_v[2 * at_x + 1]], 0))
         kinds = [filtered[96 * i : 96 * (i + 1)] for i in range(4)]
         for j in (0, 2):
-            along = left3(yb[1], cat([kinds[j][:, :LANES], kinds[j + 1][:, :LANES]], 1), NN)
+            along = left3(yb(1), cat([kinds[j][:, :LANES], kinds[j + 1][:, :LANES]], 1), NN)
             for i in range(2):
                 k = 4 * q + j + i
-                whole = left3(yb[0], kinds[j + i], NN)
+                whole = left3(yb(0), kinds[j + i], NN)
                 w2[column(k), :] = whole[:, :LANES]
                 w0[column(k), :] = whole[:, LANES:]
                 w1[column(k), :] = along[:, i * LANES : (i + 1) * LANES]
 
+    loop(FLUX_FIRST, 4, flux_z)
+    pass_on(0)
     back_y(other, side, 0)
+    loop(PAIRS // 2 - FLUX_FIRST, 4, lambda t: flux_z(t + FLUX_FIRST))
+    pass_on(1)
     back_y(other, side, 1)
+    pass_copies[0].wait_recv()
+    back_y(partner, 1 - side, 0)
     pass_on(2)
     back_y(other, side, 2)
-    for t in range(SIDE_QUADS):
+    for t in (1, 2):
         pass_copies[t].wait_recv()
         back_y(partner, 1 - side, t)
 
     tangent = side == 0
-    wave = jnp.clip(wave_ref[0] - 1, 0, 3)
+    wave = wave_ref[0]
+
+    def force(p):
+        lane = lax.broadcasted_iota(jnp.int32, (1, LANES), 1)
+        y = 2 * p + jnp.where(lane < 64, 0, 1)
+        return forcing_amp * quarter_sine(lax.rem(wave * y, N))
 
     def grid_space(t):
         third = left3(
-            zb[1], cat([w2[pair_rows(2 * t + i), :] for i in range(2)], 1), NN
+            zb(1), cat([w2[pair_rows(2 * t + i), :] for i in range(2)], 1), NN
         ).T
+        driven_pair = []
         for i in range(2):
             p = 2 * t + i
             state = state_v[:, :, lanes(p)]
             base = base_v[:, :, lanes(p)]
-            pair = left3(zb[0], cat([w0[pair_rows(p), :], w1[pair_rows(p), :]], 1), NN).T
+            pair = left3(zb(0), cat([w0[pair_rows(p), :], w1[pair_rows(p), :]], 1), NN).T
             grad = [
                 pair[:96].reshape(base.shape),
                 pair[LANES : LANES + 96].reshape(base.shape),
@@ -887,14 +968,16 @@
                     total = total + jnp.where(tangent, grad[b][a], grad[a][b]) * state[b]
                     drive = drive + grad[b][a] * base[b]
                 if a == 0:
-                    drive = drive - force[wave, :, lanes(p)]
+                    drive = drive - force(p)
                 coupled.append(-time_step * total)
                 driven.append(base[a] - time_step * drive)
-            out = left3(wz[at_z, 0], wide_rows(cat(coupled, 0), cat(driven, 0)), NT)
-            wa[pair_rows(p), :] = out[:, :LANES]
-            wb[pair_rows(p), :] = out[:, LANES:]
-
-    loop(PAIRS // 2, 2, grid_space)
+            held_coupled[:, lanes(p)] = cat(coupled, 0)
+            driven_pair.append(cat(driven, 0))
+        out = left3(wz(0), wide_rows(*driven_pair), NT)
+        for i in range(2):
+            wd[pair_rows(2 * t + i), :] = out[:, i * LANES : (i + 1) * LANES]
+
+    loop(PAIRS // 2, 4, grid_space)
 
     waves = plane_waves()
     keep = jnp.where(jnp.abs(waves[0]) <= cut_x.astype(f32), 1.0, 0.0)
@@ -903,51 +986,88 @@
         high, low = split(plane)
         return [high[:MP], low[:MP], high[MP:], low[MP:], high[:MP], high[MP:]]
 
-    def emit_planes(ref, first_tile, first_k, modes, count, third):
+    row = lax.broadcasted_iota(jnp.int32, (MP, LANES), 0)
+    upper = row > THIRD
+    folded = jnp.where(upper, 0.0, jnp.where(row == 0, 1.0, 2.0))
+
+    def emit_planes(ref, start, first_k, modes, count, fold):
         new = []
         for i in range(count):
             w = projected(waves, modes[MP * i : MP * (i + 1)], first_k + i)
             new.append([keep * part for part in w])
-        if third:
-            ref[0] = new[0][2]
+        if fold is not None:
+            held = jnp.where(upper, pltpu.roll(new[0][2], THIRD + 1, 0), new[0][0])
+            new[0][0] = jnp.where(fold, held, new[0][0])
+        tiles = []
         for j in range(0, count, 2):
-            for i, tile in enumerate(pack_pair(new[j], new[j + 1])):
-                ref[first_tile + 3 * (j // 2) + i] = tile
-
-    def quad_tiles(q, pairs=2):
-        return pl.ds(0, 7) if q == 0 else pl.ds(1 + 6 * q, 3 * pairs)
+            tiles += pack_pair(new[j], new[j + 1])
+        rows = QUAD_ROWS if count == 4 else PAIR_ROWS
+        ref[start : start + rows, :] = pack_quad(tiles)
+
+    def base_copy(t, rows):
+        rows = pl.ds(QUAD_ROWS * t, rows)
+        return remote(
+            base_send.at[rows], base_recv.at[rows], base_send_sem.at[t], base_recv_sem.at[t],
+            far,
+        )
+
+    def each_side(copies, act):
+        if len(copies) == 1:
+            act(copies[0])
+        else:
+            pl.when(side == 0)(lambda: act(copies[0]))
+            pl.when(side == 1)(lambda: act(copies[1]))
 
     base_copies = []
     for t in range(SIDE_QUADS):
         q = SIDE_QUADS * side + t
         deep = []
         for j in (0, 2):
-            both_planes = left3(wy[at_y, 0], two_columns(wb, 4 * q + j), NN)
+            both_planes = left3(wy(0), two_columns(wd, 4 * q + j), NN)
             for i in range(2):
                 deep.append(cat(ahead_deep(both_planes[:, i * LANES : (i + 1) * LANES]), 1))
-        modes = matmul(cat(deep, 0), xt[: 6 * LANES])
-        emit_planes(base_send, 1 + 6 * t, 4 * q, modes, 4, t == 0)
-        rows = quad_tiles(t)
-        copy = remote(
-            base_send.at[rows], base_recv.at[rows], base_send_sem.at[t], base_recv_sem.at[t],
-            far,
-        )
-        copy.start()
-        base_copies.append(copy)
+        modes = matmul(cat(deep, 0), flat(xt[:8]))
+        emit_planes(base_send, QUAD_ROWS * t, 4 * q, modes, 4, side == 0 if t == 0 else None)
+        copies = [base_copy(t, QUAD_ROWS)]
+        if t == SIDE_QUADS - 1:
+            copies.append(base_copy(t, PAIR_ROWS))
+        base_copies.append(copies)
+        each_side(copies, lambda copy: copy.start())
+
+    def flux_y(t):
+        k = 2 * t
+        extra = left3(wy(1), two_columns(wb, k), NN)
+        for i in range(2):
+            whole = left3(
+                wy(0), cat([wa[column(k + i), :], wc[column(k + i), :]], 1), NN
+            )
+            g[k + i] = whole[:, :LANES] + extra[:, i * LANES : (i + 1) * LANES]
+            f[k + i] = whole[:, LANES:]
+
+    loop(QK // 2, 4, flux_y)
+
+    def coupled_z(t):
+        rows = [held_coupled[:, lanes(2 * t + i)] for i in range(2)]
+        out = left3(wz(0), wide_rows(*rows), NT)
+        for i in range(2):
+            wa[pair_rows(2 * t + i), :] = out[:, i * LANES : (i + 1) * LANES]
+
+    loop(PAIRS // 2, 4, coupled_z)
 
     state_copies = []
     for q in range(STATE_QUADS):
         pairs = 2 if q < STATE_QUADS - 1 else 1
         deep = []
         for j in range(0, 2 * pairs, 2):
-            both_planes = left3(wy[at_y, 0], two_columns(wa, 4 * q + j), NN)
+            both_planes = left3(wy(0), two_columns(wa, 4 * q + j), NN)
             for i in range(2):
                 k = 4 * q + j + i
                 total = g[k] + both_planes[:, i * LANES : (i + 1) * LANES]
                 deep.append(cat(ahead_deep(total) + ahead_deep(f[k]), 1))
-        modes = matmul(cat(deep, 0), xt[...])
-        emit_planes(state_send, 1 + 6 * q, 4 * q, modes, 2 * pairs, q == 0)
-        rows = quad_tiles(q, pairs)
+        modes = matmul(cat(deep, 0), flat(xt[...]))
+        fold = True if q == 0 else None
+        emit_planes(state_send, QUAD_ROWS * q, 4 * q, modes, 2 * pairs, fold)
+        rows = pl.ds(QUAD_ROWS * q, QUAD_ROWS if pairs == 2 else PAIR_ROWS)
         copy = remote(
             state_send.at[rows], state_recv.at[rows], state_send_sem.at[q],
             state_recv_sem.at[q], far,
@@ -955,7 +1075,8 @@
         copy.start()
         state_copies.append(copy)
 
-    def spectral(tiles, third, first_k, table_ref, work):
+    def spectral(held, fold, first_k, table_ref, work):
+        tiles = unpack_quad(held)
         deep = []
         wave_x, wave_y = waves
         for j in range(len(tiles) // 3):
@@ -963,29 +1084,34 @@
                 k = jnp.asarray(first_k + 2 * j + i, jnp.int32)
                 inverse = 1.0 / jnp.maximum(k, 1).astype(f32)
                 m2 = -(wave_x * m0 + wave_y * m1) * inverse
-                if third is not None and j == 0 and i == 0:
-                    m2 = jnp.where(k == 0, third, m2)
+                if fold is not None and i == 0 and j == 0:
+                    third = pltpu.roll(m0, MP - THIRD - 1, 0)
+                    m2 = jnp.where(fold, folded * third, m2)
+                    m0 = jnp.where(fold, folded * m0, m0)
+                    m1 = jnp.where(fold, folded * m1, m1)
                 high, low = split(cat([m0, m1, m2], 1))
                 deep.append(cat([high, low, high], 1))
-        rows = matmul(cat(deep, 0), table_ref[...])
+        rows = matmul(cat(deep, 0), flat(table_ref[...]))
         planes = []
         for i in range(len(deep)):
             mine = rows[MP * i : MP * (i + 1)]
             planes.append(cat([mine[:, :LANES], mine[:, LANES:]], 0))
         for j in range(0, len(deep), 2):
-            out = left3(yb[0], cat(planes[j : j + 2], 1), NN)
+            out = left3(yb(0), cat(planes[j : j + 2], 1), NN)
             for i in range(2):
                 work[column(first_k + j + i), :] = out[:, i * LANES : (i + 1) * LANES]
 
     span = base_sum.shape[0] // 2
     sum_copies = []
     for t in range(SIDE_QUADS):
-        base_copies[t].wait_recv()
-        for i in range(7 if t == 0 else 6):
-            tile = i if t == 0 else 1 + 6 * t + i
-            base_sum[span * side + tile] = base_send[tile] + base_recv[tile]
-        start = 0 if t == 0 else 1 + 6 * t
-        rows = pl.ds(span * side + start, 7 if t == 0 else 6)
+        each_side(base_copies[t], lambda copy: copy.wait_recv())
+        mine = slice(QUAD_ROWS * t, QUAD_ROWS * (t + 1))
+        total = base_send[mine, :] + base_recv[mine, :]
+        if t == SIDE_QUADS - 1:
+            place = lax.broadcasted_iota(jnp.int32, total.shape, 0)
+            total = jnp.where((side == 0) | (place < PAIR_ROWS), total, 0.0)
+        rows = pl.ds(pl.multiple_of(span * side + QUAD_ROWS * t, 8), QUAD_ROWS)
+        base_sum[rows, :] = total
         copy = remote(
             base_sum.at[rows], base_sum.at[rows], sum_send.at[t], sum_recv.at[t], twin
         )
@@ -993,10 +1119,9 @@
         sum_copies.append(copy)
 
     def base_back(place, t):
-        first = span * place
-        tiles = [base_sum[first + 1 + 6 * t + i] for i in range(6)]
-        third = base_sum[first] if t == 0 else None
-        spectral(tiles, third, 4 * (SIDE_QUADS * place + t), xb, w0)
+        rows = pl.ds(pl.multiple_of(span * place + QUAD_ROWS * t, 8), QUAD_ROWS)
+        fold = place == 0 if t == 0 else None
+        spectral(base_sum[rows, :], fold, 4 * (SIDE_QUADS * place + t), xb, w0)
 
     for t in range(SIDE_QUADS):
         base_back(side, t)
@@ -1004,38 +1129,39 @@
         sum_copies[t].wait_recv()
         base_back(1 - side, t)
 
+    def finish_base(p):
+        rows = left3(zb(0), w0[pair_rows(p), :], NN).T
+        out_base[:, :, lanes(p)] = rows[:48].reshape(3, half, LANES)
+
+    loop(PAIRS, 8, finish_base)
+
     for q in range(STATE_QUADS):
         state_copies[q].wait_recv()
-        count = 6 if q < STATE_QUADS - 1 else 3
-        both_tiles = lambda tile: state_send[tile] + state_recv[tile]
-        tiles = [both_tiles(1 + 6 * q + i) for i in range(count)]
-        spectral(tiles, both_tiles(0) if q == 0 else None, 4 * q, xs, wc)
-
-    for copy in near_copies:
-        copy.wait_recv()
-
-    def finish_z(p):
-        rows = left3(zb[0], cat([wc[pair_rows(p), :], w0[pair_rows(p), :]], 1), NN).T
+        rows = QUAD_ROWS if q < STATE_QUADS - 1 else PAIR_ROWS
+        mine = slice(QUAD_ROWS * q, QUAD_ROWS * q + rows)
+        total = state_send[mine, :] + state_recv[mine, :]
+        spectral(total, True if q == 0 else None, 4 * q, xs, wc)
+
+    def finish_state(p):
+        rows = left3(zb(0), wc[pair_rows(p), :], NN).T
         near = near_state[:, :, lanes(p)]
         out_state[:, :, lanes(p)] = rows[:96].reshape(near.shape) - near
-        near = near_base[:, :, lanes(p)]
-        out_base[:, :, lanes(p)] = rows[LANES : LANES + 48].reshape(near.shape) - near
-
-    out_copies = []
-    for i in range(4):
-        loop(PAIRS // 4, 4, lambda p, i=i: finish_z(p + i * (PAIRS // 4)))
-        for j, (src, dst) in enumerate(((out_state, state_gap_hbm), (out_base, base_gap_hbm))):
-            copy = pltpu.make_async_copy(
-                quarter_of(src, i), quarter_of(dst, i), out_sem.at[2 * i + j]
-            )
-            copy.start()
-            out_copies.append(copy)
-
-    sent = near_copies + share_copies + pass_copies + base_copies + sum_copies + state_copies
+
+    near_copies[0].wait_recv()
+    loop(PAIRS, 8, finish_state)
+
+    def base_difference(i):
+        span = pl.ds(pl.multiple_of(i * 512, 512), 512)
+        out_base[:, :, span] -= near_base[:, :, span]
+
+    near_copies[1].wait_recv()
+    loop(N * N // 512, 4, base_difference)
+
+    sent = near_copies + share_copies + pass_copies + sum_copies + state_copies
     for copy in sent:
         copy.wait_send()
-    for copy in out_copies:
-        copy.wait()
+    for copies in base_copies:
+        each_side(copies, lambda copy: copy.wait_send())
 
 
 def fused_body(base, state, wavenumber, cutoff):
@@ -1043,44 +1169,38 @@
     rows = base.shape[1]
     half = rows // lax.axis_size("comp")
     slabs = lax.axis_size("slab")
-    tables = [
-        z_tables(), y_tables(), filter_tables(slabs), ahead_tables(slabs), behind_tables(slabs),
-        behind_tables(2 * slabs), y_back(), z_back(), force_table(),
-    ]
-    tables = [jnp.asarray(t) for t in tables]
+    tables = [jnp.asarray(np.concatenate(group)) for group in table_groups()]
     hbm = pl.BlockSpec(memory_space=pltpu.HBM)
     smem = pl.BlockSpec(memory_space=pltpu.SMEM)
     vmem = lambda *shape: pltpu.VMEM(shape, f32)
     dma = lambda count: pltpu.SemaphoreType.DMA((count,))
-    held = lambda t: pltpu.VMEM(t.shape, t.dtype)
-    held_one = lambda t: pltpu.VMEM(t.shape[1:], t.dtype)
-    wz, wy, pd, xt, xs, xb, yb, zb, force = tables
+    wide, narrow = table_places()
+    wz, wy, yb, zb, xt = (pltpu.VMEM((entry[1], 2 * MP, 3 * LANES), bf16) for entry in wide)
+    pd, xs, xb = (pltpu.VMEM((entry[1], 3 * LANES, 2 * LANES), bf16) for entry in narrow)
     work = vmem(2 * N * KP, LANES)
-    share = vmem(3 * SIDE_QUADS, 2 * MP, LANES)
+    share = vmem(3 * SIDE_QUADS, 2 * BODY + 8, LANES)
     planes = vmem(QK, 2 * MP, LANES)
-    base_tiles = vmem(1 + 6 * SIDE_QUADS, MP, LANES)
-    state_tiles = vmem(4 + 6 * (STATE_QUADS - 1), MP, LANES)
+    base_tiles = vmem(SIDE_QUADS * QUAD_ROWS, LANES)
+    state_tiles = vmem((STATE_QUADS - 1) * QUAD_ROWS + PAIR_ROWS, LANES)
     base_half = vmem(3, half, N * N)
     whole = vmem(3, rows, N * N)
     scratch = [
-        whole, whole, base_half, whole, held(wz), held(wy), held_one(pd), held_one(xt),
-        held_one(xs), held_one(xb), held(yb), held(zb), held(force),
-        *[work] * 6, planes, share, share, share, planes, planes,
-        base_tiles, base_tiles, vmem(2 + 12 * SIDE_QUADS, MP, LANES), state_tiles, state_tiles,
-        base_half, whole,
-        dma(14), dma(8), dma(2), dma(2), *[dma(SIDE_QUADS)] * 8, *[dma(STATE_QUADS)] * 2,
+        whole, whole, base_half, whole, wz, wy, pd, xt, xs, xb, yb, zb,
+        *[work] * 7, vmem(3 * rows, N * N), planes, share, share, share, planes, planes,
+        base_tiles, base_tiles, vmem(2 * SIDE_QUADS * QUAD_ROWS, LANES), state_tiles, state_tiles,
+        dma(14), dma(2), dma(2), *[dma(SIDE_QUADS)] * 8, *[dma(STATE_QUADS)] * 2,
     ]
     base_gap, state_gap = pl.pallas_call(
         fused,
-        out_shape=(
+        out_shape=[
             jax.ShapeDtypeStruct((3, half, N * N), f32),
             jax.ShapeDtypeStruct((3, rows, N * N), f32),
-        ),
-        in_specs=[hbm, hbm, smem, smem, *[hbm] * len(tables)],
-        out_specs=(hbm, hbm),
+        ],
+        in_specs=[hbm, hbm, smem, smem, hbm, hbm],
+        out_specs=[pl.BlockSpec(memory_space=pltpu.VMEM)] * 2,
         scratch_shapes=scratch,
         compiler_params=pltpu.CompilerParams(
-            vmem_limit_bytes=56 * 2**20, collective_id=0, has_side_effects=True
+            vmem_limit_bytes=51 * 2**20, collective_id=0, has_side_effects=True
         ),
         cost_estimate=pl.CostEstimate(flops=10**10, bytes_accessed=10**7, transcendentals=0),
     )(base, state, cutoff, wavenumber, *tables)

time: 72.7 us -> 62.8 us (0.86)
  Pallas kernels: 67.9 us -> 58.7 us
    pallas_call x1, Pallas kernels: 67.9 us -> 58.7 us  [fused_body(): pl.pallas_call(fused, out_shape=[jax.ShapeDtypeStruct((3, half, N * N), f...]
where the time goes in v2:
time: 62.8 us; the launch traced here: 62.7 us
  Pallas kernels  58.7 us (93%)
  local copies, waits for them, and re-layouts  2.67 us (4%)
  between operations  1.29 us (2%)
    pallas_call x1, Pallas kernels, fused_body(): pl.pallas_call(fused, out_shape=[jax.ShapeDtypeStruct((3, half, N * N), f...  58.7 us
    unnamed x4, local copies, waits for them, and re-layouts  2.67 us

profile of v2, /device:TPU:0, one launch (start us, length us, event | category | flops | bytes accessed | tf_op | source)
XLA Modules:
  0.0 62.7 jit_solution(15150698291449182893)
XLA Ops:
  1.3 0.0 copy-start
  1.3 0.6 %copy-done = s32[3]{0:T(128)S(1)} copy-done((s32[3]{0:T(128)S(1)}, s32[3]{0:T(128)}, u32[]{:S(2)}) %copy-start) | copy-done | bytes 36
  1.9 58.7 %shard_map.77 = (f32[3,16,4096]{2,1,0:T(8,128)S(1)}, f32[3,32,4096]{2,1,0:T(8,128)S(1)}) custom-call(f32[3,32,4096]{2,1,0:T(8,128)} %bitcast.6, f32[3,32,4096]{2,1,0:T(8,128)} %bitcast.7, s32[3]{0:T(128)S(1)} %copy-done, s32[1]{0:T(128)S(6)} %copy.10.wave_ref, bf16[56,96,384]{2,1,0:T(8,128)(2,1)} %constant.4.clone.wide_hbm, ...), custom_call_target="tpu_custom_call" | custom-call | flops 10000000000 | bytes 10000000 | tf_op jit(solution)/shard_map/pallas_call | solution.py:1193
  60.7 0.9 %copy.11 = f32[1,3,16,4096]{3,2,1,0:T(8,128)} copy(f32[1,3,16,4096]{3,2,1,0:T(8,128)S(1)} %bitcast.5) | data formatting | bytes 1572864
  61.5 1.1 %copy.12 = f32[1,1,3,32,4096]{4,3,2,1,0:T(8,128)} copy(f32[1,1,3,32,4096]{4,3,2,1,0:T(8,128)S(1)} %bitcast.4) | data formatting | bytes 3145728
Async XLA Ops:
  1.3 0.7 %copy-start = (s32[3]{0:T(128)S(1)}, s32[3]{0:T(128)}, u32[]{:S(2)}) copy-start(s32[3]{0:T(128)} %cutoff_ref.1) | copy-start | bytes 40

commit v3 on v2

--- a/solution.py
+++ b/solution.py
@@ -752,8 +752,8 @@
 
 
 def fused(
-    base_hbm, state_hbm, cutoff_ref, wave_ref, wide_hbm, narrow_hbm, out_base, out_state,
-    base_v, state_v, near_base, near_state, wz_v, wy_v, pd_v, xt, xs, xb, yb_v, zb_v,
+    base_hbm, state_hbm, cutoff_hbm, wave_ref, wide_hbm, narrow_hbm, out_base, out_state,
+    base_v, state_v, near_base, near_state, cutoff_ref, wz_v, wy_v, pd_v, xt, xs, xb, yb_v, zb_v,
     w0, w1, w2, wa, wb, wc, wd, held_coupled, own, share, other, partner, g, f,
     base_send, base_recv, base_sum, state_send, state_recv, local_sem, near_send, near_recv, share_send, share_recv, pass_send, pass_recv,
     base_send_sem, base_recv_sem, sum_send, sum_recv, state_send_sem, state_recv_sem,
@@ -792,6 +792,8 @@
         start, rows = entry
         return hbm.at[pl.ds(start + rows * index, rows)], dst
 
+    cut_copy = local(13, cutoff_hbm, cutoff_ref)
+    cut_copy.start()
     wz_copy = local(0, *table_part(wide_hbm, wide_places[0], 0, wz_v))
     base_copies = [
         local(1 + i, quarter_of(base_hbm, i), quarter_of(base_v, i)) for i in range(4)
@@ -809,37 +811,6 @@
     for copy in (wz_copy, *base_copies, wy_copy, state_copy):
         copy.start()
 
-    cut_x, cut_y, cut_z = (cutoff_ref[i] for i in range(3))
-    at_x, at_y, at_z = (jnp.clip(cut - LOW, 0, THIRD - LOW) for cut in (cut_x, cut_y, cut_z))
-
-    def back_table(ref, kind, depth):
-        return ref[2 * kind : 2 * kind + 2].reshape(4 * MP, 3 * LANES)[: 2 * N, :depth]
-
-    wz = lambda kind: wz_v[2 * at_z + kind]
-    wy = lambda kind: wy_v[2 * at_y + kind]
-    yb = lambda kind: back_table(yb_v, kind, 6 * MP)
-    zb = lambda kind: back_table(zb_v, kind, 12 * KP)
-
-    def base_ahead_z(p):
-        w0[pair_rows(p), :] = left3(wz(0), wide_rows(flat(base_v[:, :, lanes(p)])), NT)
-
-    wz_copy.wait()
-    for i, copy in enumerate(base_copies):
-        copy.wait()
-        loop(PAIRS // 4, Z1, lambda p, i=i: base_ahead_z(p + i * (PAIRS // 4)))
-    for copy in late_copies:
-        copy.start()
-    wy_copy.wait()
-
-    def base_planes(q):
-        planes = []
-        for j in (0, 2):
-            both_planes = left3(wy(0), two_columns(w0, 4 * q + j), NN)
-            planes += [both_planes[:, :LANES], both_planes[:, LANES:]]
-        for i in range(4):
-            own[4 * q + i] = planes[i]
-        return planes
-
     near_copies = [
         remote(
             state_hbm, near_state, near_send.at[0], near_recv.at[0],
@@ -850,14 +821,46 @@
             near_recv.at[1], {"seg": before},
         ),
     ]
+    cut_copy.wait()
+    cut_x, cut_y, cut_z = (cutoff_ref[i] for i in range(3))
+    at_x, at_y, at_z = (jnp.clip(cut - LOW, 0, THIRD - LOW) for cut in (cut_x, cut_y, cut_z))
+
+    def back_table(ref, kind, depth):
+        return ref[2 * kind : 2 * kind + 2].reshape(4 * MP, 3 * LANES)[: 2 * N, :depth]
+
+    wz = lambda kind: wz_v[2 * at_z + kind]
+    wy = lambda kind: wy_v[2 * at_y + kind]
+    yb = lambda kind: back_table(yb_v, kind, 6 * MP)
+    zb = lambda kind: back_table(zb_v, kind, 12 * KP)
+
+    def base_ahead_z(p):
+        w0[pair_rows(p), :] = left3(wz(0), wide_rows(flat(base_v[:, :, lanes(p)])), NT)
+
+    wz_copy.wait()
+    for i, copy in enumerate(base_copies):
+        copy.wait()
+        loop(PAIRS // 4, Z1, lambda p, i=i: base_ahead_z(p + i * (PAIRS // 4)))
+        if i == 0:
+            pl.semaphore_wait(barrier, 4)
+            for near_copy in near_copies:
+                near_copy.start()
+    for copy in late_copies:
+        copy.start()
+    wy_copy.wait()
+
+    def base_planes(q):
+        planes = []
+        for j in (0, 2):
+            both_planes = left3(wy(0), two_columns(w0, 4 * q + j), NN)
+            planes += [both_planes[:, :LANES], both_planes[:, LANES:]]
+        for i in range(4):
+            own[4 * q + i] = planes[i]
+        return planes
+
     share_copies = []
     for t in range(SIDE_QUADS):
         for i, tile in enumerate(pack_share(base_planes(SIDE_QUADS * side + t))):
             share[3 * t + i] = tile
-        if t == 0:
-            pl.semaphore_wait(barrier, 4)
-            for copy in near_copies:
-                copy.start()
         rows = pl.ds(3 * t, 3)
         copy = remote(
             share.at[rows], other.at[rows], share_send.at[t], share_recv.at[t], far
@@ -1164,6 +1167,28 @@
         each_side(copies, lambda copy: copy.wait_send())
 
 
+def copy_out(base_v, state_v, base_hbm, state_hbm, sem):
+    copies = [
+        pltpu.make_async_copy(base_v, base_hbm, sem.at[0]),
+        pltpu.make_async_copy(state_v, state_hbm, sem.at[1]),
+    ]
+    for copy in copies:
+        copy.start()
+    for copy in copies:
+        copy.wait()
+
+
+def write_out(*fields):
+    return pl.pallas_call(
+        copy_out,
+        out_shape=[jax.ShapeDtypeStruct(field.shape, f32) for field in fields],
+        in_specs=[pl.BlockSpec(memory_space=pltpu.VMEM)] * 2,
+        out_specs=[pl.BlockSpec(memory_space=pltpu.HBM)] * 2,
+        scratch_shapes=[pltpu.SemaphoreType.DMA((2,))],
+        compiler_params=pltpu.CompilerParams(vmem_limit_bytes=2**20),
+    )(*fields)
+
+
 def fused_body(base, state, wavenumber, cutoff):
     base, state = base[0], state[0, 0]
     rows = base.shape[1]
@@ -1185,7 +1210,7 @@
     base_half = vmem(3, half, N * N)
     whole = vmem(3, rows, N * N)
     scratch = [
-        whole, whole, base_half, whole, wz, wy, pd, xt, xs, xb, yb, zb,
+        whole, whole, base_half, whole, pltpu.SMEM((3,), jnp.int32), wz, wy, pd, xt, xs, xb, yb, zb,
         *[work] * 7, vmem(3 * rows, N * N), planes, share, share, share, planes, planes,
         base_tiles, base_tiles, vmem(2 * SIDE_QUADS * QUAD_ROWS, LANES), state_tiles, state_tiles,
         dma(14), dma(2), dma(2), *[dma(SIDE_QUADS)] * 8, *[dma(STATE_QUADS)] * 2,
@@ -1196,7 +1221,7 @@
             jax.ShapeDtypeStruct((3, half, N * N), f32),
             jax.ShapeDtypeStruct((3, rows, N * N), f32),
         ],
-        in_specs=[hbm, hbm, smem, smem, hbm, hbm],
+        in_specs=[hbm, hbm, hbm, smem, hbm, hbm],
         out_specs=[pl.BlockSpec(memory_space=pltpu.VMEM)] * 2,
         scratch_shapes=scratch,
         compiler_params=pltpu.CompilerParams(
@@ -1204,6 +1229,7 @@
         ),
         cost_estimate=pl.CostEstimate(flops=10**10, bytes_accessed=10**7, transcendentals=0),
     )(base, state, cutoff, wavenumber, *tables)
+    base_gap, state_gap = write_out(base_gap, state_gap)
     return base_gap[None], state_gap[None, None]
 
 

time: 62.8 us -> 60.3 us (0.960)
  local copies, waits for them, and re-layouts: 2.67 us -> 0.65 us
    pallas_call x1, Pallas kernels: 58.7 us -> 56.6 us  [fused_body(): pl.pallas_call(fused, out_shape=[jax.ShapeDtypeStruct((3, half, N * N), f...]
    unnamed x4 -> x2, local copies, waits for them, and re-layouts: 2.67 us -> 0.65 us
    pallas_call x0 -> x1, Pallas kernels: none -> 1.42 us  [write_out(): pl.pallas_call(copy_out, out_shape=[jax.ShapeDtypeStruct(field.shape, f32...]
where the time goes in v3:
time: 60.3 us; the launch traced here: 60.2 us
  Pallas kernels  58.1 us (96%)
  between operations  1.45 us (2%)
  local copies, waits for them, and re-layouts  0.65 us (1%)
    pallas_call x1, Pallas kernels, fused_body(): pl.pallas_call(fused, out_shape=[jax.ShapeDtypeStruct((3, half, N * N), f...  56.6 us
    pallas_call x1, Pallas kernels, write_out(): pl.pallas_call(copy_out, out_shape=[jax.ShapeDtypeStruct(field.shape, f32...  1.42 us

profile of v3, /device:TPU:0, one launch (start us, length us, event | category | flops | bytes accessed | tf_op | source)
XLA Modules:
  0.0 60.2 jit_solution(14906967637584337439)
XLA Ops:
  1.3 0.0 copy-start
  1.3 0.6 %copy-done = s32[3]{0:T(128)S(1)} copy-done((s32[3]{0:T(128)S(1)}, s32[3]{0:T(128)}, u32[]{:S(2)}) %copy-start) | copy-done | bytes 36
  1.9 56.6 %shard_map.77 = (f32[3,16,4096]{2,1,0:T(8,128)S(1)}, f32[3,32,4096]{2,1,0:T(8,128)S(1)}) custom-call(f32[3,32,4096]{2,1,0:T(8,128)} %bitcast.4, f32[3,32,4096]{2,1,0:T(8,128)} %bitcast.5, s32[3]{0:T(128)S(1)} %copy-done, s32[1]{0:T(128)S(6)} %copy.8.wave_ref, bf16[56,96,384]{2,1,0:T(8,128)(2,1)} %constant.4.clone.wide_hbm, ...), custom_call_target="tpu_custom_call" | custom-call | flops 10000000000 | bytes 10000000 | tf_op jit(solution)/shard_map/pallas_call | solution.py:1218
  58.6 1.4 %shard_map.78 = (f32[3,16,4096]{2,1,0:T(8,128)}, f32[3,32,4096]{2,1,0:T(8,128)}) custom-call(f32[3,16,4096]{2,1,0:T(8,128)S(1)} %get-tuple-element.6.base_v, f32[3,32,4096]{2,1,0:T(8,128)S(1)} %get-tuple-element.7.state_v), custom_call_target="tpu_custom_call" | custom-call | tf_op jit(solution)/shard_map/pallas_call | solution.py:1182
Async XLA Ops:
  1.3 0.7 %copy-start = (s32[3]{0:T(128)S(1)}, s32[3]{0:T(128)}, u32[]{:S(2)}) copy-start(s32[3]{0:T(128)} %cutoff_hbm.1) | copy-start | bytes 40

commit v4 on v3

--- a/solution.py
+++ b/solution.py
@@ -536,7 +536,7 @@
 QK = 24
 SIDE_QUADS = 3
 STATE_QUADS = 6
-FLUX_FIRST = 8
+FLUX_FIRST = 12
 
 
 def lane_pad(values, axis, size=LANES):
@@ -812,13 +812,16 @@
         copy.start()
 
     near_copies = [
+        *[
+            remote(
+                quarter_of(state_hbm, i), quarter_of(near_state, i), near_send.at[1 + i],
+                near_recv.at[1 + i], {"seg": jnp.where(side == 0, before, after)},
+            )
+            for i in range(4)
+        ],
         remote(
-            state_hbm, near_state, near_send.at[0], near_recv.at[0],
-            {"seg": jnp.where(side == 0, before, after)},
-        ),
-        remote(
-            base_hbm.at[:, pl.ds(half * side, half), :], near_base, near_send.at[1],
-            near_recv.at[1], {"seg": before},
+            base_hbm.at[:, pl.ds(half * side, half), :], near_base, near_send.at[0],
+            near_recv.at[0], {"seg": before},
         ),
     ]
     cut_copy.wait()
@@ -836,14 +839,13 @@
     def base_ahead_z(p):
         w0[pair_rows(p), :] = left3(wz(0), wide_rows(flat(base_v[:, :, lanes(p)])), NT)
 
+    pl.semaphore_wait(barrier, 4)
+    for near_copy in near_copies:
+        near_copy.start()
     wz_copy.wait()
     for i, copy in enumerate(base_copies):
         copy.wait()
         loop(PAIRS // 4, Z1, lambda p, i=i: base_ahead_z(p + i * (PAIRS // 4)))
-        if i == 0:
-            pl.semaphore_wait(barrier, 4)
-            for near_copy in near_copies:
-                near_copy.start()
     for copy in late_copies:
         copy.start()
     wy_copy.wait()
@@ -926,7 +928,7 @@
                 w0[column(k), :] = whole[:, LANES:]
                 w1[column(k), :] = along[:, i * LANES : (i + 1) * LANES]
 
-    loop(FLUX_FIRST, 4, flux_z)
+    loop(FLUX_FIRST, 6, flux_z)
     pass_on(0)
     back_y(other, side, 0)
     loop(PAIRS // 2 - FLUX_FIRST, 4, lambda t: flux_z(t + FLUX_FIRST))
@@ -980,7 +982,7 @@
         for i in range(2):
             wd[pair_rows(2 * t + i), :] = out[:, i * LANES : (i + 1) * LANES]
 
-    loop(PAIRS // 2, 4, grid_space)
+    loop(PAIRS // 2, 8, grid_space)
 
     waves = plane_waves()
     keep = jnp.where(jnp.abs(waves[0]) <= cut_x.astype(f32), 1.0, 0.0)
@@ -1147,17 +1149,23 @@
 
     def finish_state(p):
         rows = left3(zb(0), wc[pair_rows(p), :], NN).T
-        near = near_state[:, :, lanes(p)]
-        out_state[:, :, lanes(p)] = rows[:96].reshape(near.shape) - near
-
-    near_copies[0].wait_recv()
-    loop(PAIRS, 8, finish_state)
+        out_state[:, :, lanes(p)] = rows[:96].reshape(3, 2 * half, LANES)
+
+    loop(PAIRS, 16, finish_state)
+
+    def state_difference(i):
+        span = pl.ds(pl.multiple_of(i * 512, 512), 512)
+        out_state[:, :, span] -= near_state[:, :, span]
+
+    for i in range(4):
+        near_copies[i].wait_recv()
+        loop(2, 2, lambda j, i=i: state_difference(2 * i + j))
 
     def base_difference(i):
         span = pl.ds(pl.multiple_of(i * 512, 512), 512)
         out_base[:, :, span] -= near_base[:, :, span]
 
-    near_copies[1].wait_recv()
+    near_copies[4].wait_recv()
     loop(N * N // 512, 4, base_difference)
 
     sent = near_copies + share_copies + pass_copies + sum_copies + state_copies
@@ -1213,7 +1221,7 @@
         whole, whole, base_half, whole, pltpu.SMEM((3,), jnp.int32), wz, wy, pd, xt, xs, xb, yb, zb,
         *[work] * 7, vmem(3 * rows, N * N), planes, share, share, share, planes, planes,
         base_tiles, base_tiles, vmem(2 * SIDE_QUADS * QUAD_ROWS, LANES), state_tiles, state_tiles,
-        dma(14), dma(2), dma(2), *[dma(SIDE_QUADS)] * 8, *[dma(STATE_QUADS)] * 2,
+        dma(14), dma(5), dma(5), *[dma(SIDE_QUADS)] * 8, *[dma(STATE_QUADS)] * 2,
     ]
     base_gap, state_gap = pl.pallas_call(
         fused,

time: 60.3 us -> 60.1 us (level)
  no operation moved by 1% of the time
where the time goes in v4:
time: 60.1 us; the launch traced here: 60 us
  Pallas kernels  57.9 us (96%)
  between operations  1.45 us (2%)
  local copies, waits for them, and re-layouts  0.65 us (1%)
    pallas_call x1, Pallas kernels, fused_body(): pl.pallas_call(fused, out_shape=[jax.ShapeDtypeStruct((3, half, N * N), f...  56.4 us
    pallas_call x1, Pallas kernels, write_out(): pl.pallas_call(copy_out, out_shape=[jax.ShapeDtypeStruct(field.shape, f32...  1.42 us

profile of v4, /device:TPU:0, one launch (start us, length us, event | category | flops | bytes accessed | tf_op | source)
XLA Modules:
  0.0 60.0 jit_solution(6230973837174930838)
XLA Ops:
  1.3 0.0 copy-start
  1.3 0.6 %copy-done = s32[3]{0:T(128)S(1)} copy-done((s32[3]{0:T(128)S(1)}, s32[3]{0:T(128)}, u32[]{:S(2)}) %copy-start) | copy-done | bytes 36
  1.9 56.4 %shard_map.77 = (f32[3,16,4096]{2,1,0:T(8,128)S(1)}, f32[3,32,4096]{2,1,0:T(8,128)S(1)}) custom-call(f32[3,32,4096]{2,1,0:T(8,128)} %bitcast.4, f32[3,32,4096]{2,1,0:T(8,128)} %bitcast.5, s32[3]{0:T(128)S(1)} %copy-done, s32[1]{0:T(128)S(6)} %copy.8.wave_ref, bf16[56,96,384]{2,1,0:T(8,128)(2,1)} %constant.4.clone.wide_hbm, ...), custom_call_target="tpu_custom_call" | custom-call | flops 10000000000 | bytes 10000000 | tf_op jit(solution)/shard_map/pallas_call | solution.py:1226
  58.4 1.4 %shard_map.78 = (f32[3,16,4096]{2,1,0:T(8,128)}, f32[3,32,4096]{2,1,0:T(8,128)}) custom-call(f32[3,16,4096]{2,1,0:T(8,128)S(1)} %get-tuple-element.6.base_v, f32[3,32,4096]{2,1,0:T(8,128)S(1)} %get-tuple-element.7.state_v), custom_call_target="tpu_custom_call" | custom-call | tf_op jit(solution)/shard_map/pallas_call | solution.py:1190
Async XLA Ops:
  1.3 0.7 %copy-start = (s32[3]{0:T(128)S(1)}, s32[3]{0:T(128)}, u32[]{:S(2)}) copy-start(s32[3]{0:T(128)} %cutoff_hbm.1) | copy-start | bytes 40

commit v5 on v4

--- a/solution.py
+++ b/solution.py
@@ -1236,7 +1236,7 @@
             vmem_limit_bytes=51 * 2**20, collective_id=0, has_side_effects=True
         ),
         cost_estimate=pl.CostEstimate(flops=10**10, bytes_accessed=10**7, transcendentals=0),
-    )(base, state, cutoff, wavenumber, *tables)
+    )(base, state, pltpu.with_memory_space_constraint(cutoff, pltpu.HBM), wavenumber, *tables)
     base_gap, state_gap = write_out(base_gap, state_gap)
     return base_gap[None], state_gap[None, None]
 

time: 60.1 us -> 59.5 us (0.990)
  local copies, waits for them, and re-layouts: 0.65 us -> 0 us
    unnamed x2 -> x0, local copies, waits for them, and re-layouts: 0.65 us -> none
where the time goes in v5:
time: 59.5 us; the launch traced here: 59.4 us
  Pallas kernels  57.9 us (97%)
  between operations  1.44 us (2%)
    pallas_call x1, Pallas kernels, fused_body(): pl.pallas_call(fused, out_shape=[jax.ShapeDtypeStruct((3, half, N * N), f...  56.5 us
    pallas_call x1, Pallas kernels, write_out(): pl.pallas_call(copy_out, out_shape=[jax.ShapeDtypeStruct(field.shape, f32...  1.42 us

profile of v5, /device:TPU:0, one launch (start us, length us, event | category | flops | bytes accessed | tf_op | source)
XLA Modules:
  0.0 59.4 jit_solution(14861911628378465098)
XLA Ops:
  1.3 56.5 %shard_map.77 = (f32[3,16,4096]{2,1,0:T(8,128)S(1)}, f32[3,32,4096]{2,1,0:T(8,128)S(1)}) custom-call(f32[3,32,4096]{2,1,0:T(8,128)} %bitcast.4, f32[3,32,4096]{2,1,0:T(8,128)} %bitcast.5, s32[3]{0:T(128)} %cutoff_hbm.1, s32[1]{0:T(128)S(6)} %copy.8.wave_ref, bf16[56,96,384]{2,1,0:T(8,128)(2,1)} %constant.4.clone.wide_hbm, ...), custom_call_target="tpu_custom_call" | custom-call | flops 10000000000 | bytes 10000000 | tf_op jit(solution)/shard_map/pallas_call | solution.py:1226
  57.8 1.4 %shard_map.78 = (f32[3,16,4096]{2,1,0:T(8,128)}, f32[3,32,4096]{2,1,0:T(8,128)}) custom-call(f32[3,16,4096]{2,1,0:T(8,128)S(1)} %get-tuple-element.6.base_v, f32[3,32,4096]{2,1,0:T(8,128)S(1)} %get-tuple-element.7.state_v), custom_call_target="tpu_custom_call" | custom-call | tf_op jit(solution)/shard_map/pallas_call | solution.py:1190
